TPU v7x, 32 devices: a whole 2x2x4 slice. The times are simulated.
32 devices in a mesh: seq: 32 (over z, y, x, core).
Axes of the slice: x: 2, y: 2, z: 4, core: 2. Of those that a mesh axis runs over, the one named last changes fastest.
Arguments:
- tokens: bfloat16 [4, 2048, 1024], P(None, 'seq'), may hold values from -6 to 6
- gain_attn: float32 [1024], replicated, may hold values from 0.25 to 1.75
- gain_mlp: float32 [1024], replicated, may hold values from 0.25 to 1.75
- w_query: bfloat16 [1024, 1024], replicated, may hold values from -0.1875 to 0.1875
- w_key: bfloat16 [1024, 1024], replicated, may hold values from -0.1875 to 0.1875
- w_value: bfloat16 [1024, 1024], replicated, may hold values from -0.1875 to 0.1875
- w_out: bfloat16 [1024, 1024], replicated, may hold values from -1 to 1
- w_gate: bfloat16 [1024, 2752], replicated, may hold values from -0.1875 to 0.1875
- w_up: bfloat16 [1024, 2752], replicated, may hold values from -0.1875 to 0.1875
- w_down: bfloat16 [2752, 1024], replicated, may hold values from -0.109375 to 0.109375
- cotangent: bfloat16 [4, 2048, 1024], P(None, 'seq'), may hold values from -6 to 6
- lengths: int32 [4, 8], replicated, may hold values from 192 to 320, as said below
Outputs:
- output: bfloat16 [4, 2048, 1024], P(None, 'seq')
- input_grad: float32 [4, 2048, 1024], P(None, 'seq')
- grad_gain_attn: float32 [1024], replicated
- grad_gain_mlp: float32 [1024], replicated
- grad_w_query: float32 [1048576], P('seq')
- grad_w_key: float32 [1048576], P('seq')
- grad_w_value: float32 [1048576], P('seq')
- grad_w_out: float32 [1048576], P('seq')
- grad_w_gate: float32 [2818048], P('seq')
- grad_w_up: float32 [2818048], P('seq')
- grad_w_down: float32 [2818048], P('seq')
Inputs may be any that keep to these rules, and one draw needn't show every extreme that they name: `lengths`: each row sums to 2048; every row holds a length of 192 and one of 320.
All inputs are finite; a program needn't handle non-finite values.
Results may differ from a plain program's by a relative error of at most 0.013.
Values may be sent and summed in bfloat16 or wider, within the bound.
A program may use at most 320 MiB of HBM per device.

v0:
```python
import math

import jax
import jax.numpy as jnp
from jax import lax
from jax.sharding import PartitionSpec as P

HEADS = 16
HEAD = 64
WIN = 64


norm_epsilon = 1e-05


def from_behind(value, axis, steps):
    count = lax.axis_size(axis)
    leading, last = (max(0, -steps), min(count, count - steps))
    return lax.ppermute(value, axis, [(source, source + steps) for source in range(leading, last)])


def from_partner(value, axis, bit):
    return lax.ppermute(value, axis, [(i, i ^ 1 << bit) for i in range(lax.axis_size(axis))])


def outer_sum(left, right):
    return lax.dot_general(
        left, right, (((0,), (0,)), ((), ())), preferred_element_type=jnp.float32
    )


def times_transpose(left, weight):
    return lax.dot_general(
        left, weight, (((1,), (1,)), ((), ())), preferred_element_type=jnp.float32
    )


def norm_backward(grad_normed, normed, row_scale):
    return row_scale * (
        grad_normed - normed * jnp.mean(grad_normed * normed, axis=-1, keepdims=True)
    )


def band_windows(padded, blocks):
    split_rows = padded.reshape((blocks + 1, WIN) + padded.shape[1:])
    return jnp.concatenate([split_rows[:-1], split_rows[1:]], axis=1)


def fold_windows(blocked, blocks):
    lower_half = blocked[:, :WIN].reshape((blocks * WIN,) + blocked.shape[2:])
    upper_half = blocked[:, WIN:].reshape((blocks * WIN,) + blocked.shape[2:])
    zero_rows = jnp.zeros((WIN,) + blocked.shape[2:], blocked.dtype)
    return jnp.concatenate([lower_half, zero_rows], axis=0) + jnp.concatenate(
        [zero_rows, upper_half], axis=0
    )


def band_mask(length_row, start, tok_count, blocks):
    seq_ends = jnp.cumsum(length_row)
    positions = start + jnp.arange(-WIN, tok_count, dtype=jnp.int32)
    segments = jnp.sum((seq_ends[None, :] <= positions[:, None]).astype(jnp.int32), axis=1)
    key_pos = band_windows(positions, blocks)
    key_seg = band_windows(segments, blocks)
    query_pos = positions[WIN:].reshape(blocks, WIN)
    query_seg = segments[WIN:].reshape(blocks, WIN)
    offset = query_pos[:, :, None] - key_pos[:, None, :]
    return (
        (query_seg[:, :, None] == key_seg[:, None, :])
        & (offset >= 0)
        & (offset < WIN)
        & (key_pos[:, None, :] >= 0)
    )


def block_logits(query_blocks, key_blocks, allowed, score_scale):
    raw_scores = jnp.einsum(
        "bqhd,bkhd->bhqk", query_blocks, key_blocks, preferred_element_type=jnp.float32
    )
    return jnp.where(allowed[:, None], raw_scores * score_scale, -1e30)


def attend_forward(queries, key_pad, value_pad, allowed, blocks, score_scale):
    query_blocks = queries.reshape(blocks, WIN, HEADS, HEAD)
    key_blocks = band_windows(key_pad, blocks).reshape(blocks, 2 * WIN, HEADS, HEAD)
    value_blocks = band_windows(value_pad, blocks).reshape(blocks, 2 * WIN, HEADS, HEAD)
    logits = block_logits(query_blocks, key_blocks, allowed, score_scale)
    row_peak = jnp.max(logits, axis=-1, keepdims=True)
    exp_scores = jnp.exp(logits - row_peak)
    row_total = jnp.sum(exp_scores, axis=-1, keepdims=True)
    probability = (exp_scores / row_total).astype(jnp.bfloat16)
    log_total = row_peak + jnp.log(row_total)
    attended = jnp.einsum(
        "bhqk,bkhd->bqhd", probability, value_blocks, preferred_element_type=jnp.float32
    )
    attended = attended.reshape(blocks * WIN, HEADS * HEAD).astype(jnp.bfloat16)
    return (attended, log_total, (query_blocks, key_blocks, value_blocks))


def attend_backward(grad_attended, log_total, allowed, block_data, blocks, score_scale):
    query_blocks, key_blocks, value_blocks = block_data
    grad_blocks = grad_attended.reshape(blocks, WIN, HEADS, HEAD)
    logits = block_logits(query_blocks, key_blocks, allowed, score_scale)
    probability = jnp.exp(logits - log_total)
    grad_prob = jnp.einsum(
        "bqhd,bkhd->bhqk", grad_blocks, value_blocks, preferred_element_type=jnp.float32
    )
    delta_row = jnp.sum(probability * grad_prob, axis=-1, keepdims=True)
    grad_scores = (score_scale * probability * (grad_prob - delta_row)).astype(jnp.bfloat16)
    grad_query = jnp.einsum(
        "bhqk,bkhd->bqhd", grad_scores, key_blocks, preferred_element_type=jnp.float32
    )
    grad_key_blocks = jnp.einsum(
        "bhqk,bqhd->bkhd", grad_scores, query_blocks, preferred_element_type=jnp.float32
    )
    grad_value_blocks = jnp.einsum(
        "bhqk,bqhd->bkhd",
        probability.astype(jnp.bfloat16),
        grad_blocks,
        preferred_element_type=jnp.float32,
    )
    grad_query = grad_query.reshape(blocks * WIN, HEADS * HEAD).astype(jnp.bfloat16)
    grad_key_pad = fold_windows(grad_key_blocks.reshape(blocks, 2 * WIN, HEADS * HEAD), blocks)
    grad_value_pad = fold_windows(grad_value_blocks.reshape(blocks, 2 * WIN, HEADS * HEAD), blocks)
    return (grad_query, grad_key_pad, grad_value_pad)


def halving_sum(members, swap_fn):
    levels = lax.axis_size("seq").bit_length() - 1
    my_index = lax.axis_index("seq")
    current = tuple(members)
    for bit in reversed(range(levels)):
        upper_pick = my_index >> bit & 1
        kept_parts = []
        sent_parts = []
        for member in current:
            half = member.shape[0] // 2
            kept_parts.append(lax.dynamic_slice_in_dim(member, upper_pick * half, half, 0))
            sent_parts.append(lax.dynamic_slice_in_dim(member, (1 - upper_pick) * half, half, 0))
        received = swap_fn(tuple(sent_parts), bit)
        current = tuple((kept + came for kept, came in zip(kept_parts, received)))
    return current


def per_device(
    tokens,
    gain_attn,
    gain_mlp,
    w_query,
    w_key,
    w_value,
    w_out,
    w_gate,
    w_up,
    w_down,
    cotangent,
    lengths,
):
    micro_count = tokens.shape[0]
    tok_count = tokens.shape[1]
    blocks = tok_count // WIN
    score_scale = 1.0 / math.sqrt(HEAD)
    start = lax.axis_index("seq") * tok_count
    grad_query_w = jnp.zeros(w_query.shape, jnp.float32)
    grad_key_w = jnp.zeros(w_key.shape, jnp.float32)
    grad_value_w = jnp.zeros(w_value.shape, jnp.float32)
    grad_out_w = jnp.zeros(w_out.shape, jnp.float32)
    grad_gate_w = jnp.zeros(w_gate.shape, jnp.float32)
    grad_up_w = jnp.zeros(w_up.shape, jnp.float32)
    grad_down_w = jnp.zeros(w_down.shape, jnp.float32)
    grad_gain_attn = jnp.zeros_like(gain_attn)
    grad_gain_mlp = jnp.zeros_like(gain_mlp)
    outputs = []
    input_grads = []
    for micro_index in range(micro_count):
        inputs = tokens[micro_index].astype(jnp.float32)
        allowed = band_mask(lengths[micro_index], start, tok_count, blocks)
        scale_attn = lax.rsqrt(jnp.mean(inputs * inputs, axis=-1, keepdims=True) + norm_epsilon)
        normed_attn = inputs * scale_attn
        first_rows = (normed_attn * gain_attn).astype(jnp.bfloat16)
        queries = jnp.dot(first_rows, w_query, preferred_element_type=jnp.float32).astype(
            jnp.bfloat16
        )
        key_rows = jnp.dot(first_rows, w_key, preferred_element_type=jnp.float32).astype(
            jnp.bfloat16
        )
        value_rows = jnp.dot(first_rows, w_value, preferred_element_type=jnp.float32).astype(
            jnp.bfloat16
        )
        prior_keys, prior_values = from_behind((key_rows, value_rows), "seq", 1)
        key_pad = jnp.concatenate([prior_keys, key_rows], axis=0)
        value_pad = jnp.concatenate([prior_values, value_rows], axis=0)
        attended, log_total, block_data = attend_forward(
            queries, key_pad, value_pad, allowed, blocks, score_scale
        )
        middle = inputs + jnp.dot(attended, w_out, preferred_element_type=jnp.float32)
        scale_mlp = lax.rsqrt(jnp.mean(middle * middle, axis=-1, keepdims=True) + norm_epsilon)
        normed_mlp = middle * scale_mlp
        second_rows = (normed_mlp * gain_mlp).astype(jnp.bfloat16)
        gate_proj = jnp.dot(second_rows, w_gate, preferred_element_type=jnp.float32)
        up_proj = jnp.dot(second_rows, w_up, preferred_element_type=jnp.float32)
        sigmoid_gate = jax.nn.sigmoid(gate_proj)
        silu_gate = gate_proj * sigmoid_gate
        hidden = (silu_gate * up_proj).astype(jnp.bfloat16)
        outputs.append(
            (middle + jnp.dot(hidden, w_down, preferred_element_type=jnp.float32)).astype(
                jnp.bfloat16
            )
        )
        grad_output = cotangent[micro_index]
        grad_rows = grad_output.astype(jnp.float32)
        grad_down_w = grad_down_w + outer_sum(hidden, grad_output)
        grad_hidden = times_transpose(grad_output, w_down)
        grad_gate = (
            grad_hidden * up_proj * sigmoid_gate * (1.0 + gate_proj * (1.0 - sigmoid_gate))
        ).astype(jnp.bfloat16)
        grad_up = (grad_hidden * silu_gate).astype(jnp.bfloat16)
        grad_gate_w = grad_gate_w + outer_sum(second_rows, grad_gate)
        grad_up_w = grad_up_w + outer_sum(second_rows, grad_up)
        grad_second = times_transpose(grad_gate, w_gate) + times_transpose(grad_up, w_up)
        grad_gain_mlp = grad_gain_mlp + jnp.sum(grad_second * normed_mlp, axis=0)
        grad_middle = grad_rows + norm_backward(grad_second * gain_mlp, normed_mlp, scale_mlp)
        grad_branch = grad_middle.astype(jnp.bfloat16)
        grad_out_w = grad_out_w + outer_sum(attended, grad_branch)
        grad_attended = times_transpose(grad_branch, w_out).astype(jnp.bfloat16)
        grad_queries, grad_key_pad, grad_value_pad = attend_backward(
            grad_attended, log_total, allowed, block_data, blocks, score_scale
        )
        returned_keys, returned_values = (
            from_behind(grad_key_pad[:WIN].astype(jnp.bfloat16), "seq", -1).astype(jnp.float32),
            from_behind(grad_value_pad[:WIN].astype(jnp.bfloat16), "seq", -1).astype(jnp.float32),
        )
        grad_keys = grad_key_pad[WIN:].at[tok_count - WIN :].add(returned_keys).astype(jnp.bfloat16)
        grad_values = (
            grad_value_pad[WIN:].at[tok_count - WIN :].add(returned_values).astype(jnp.bfloat16)
        )
        grad_query_w = grad_query_w + outer_sum(first_rows, grad_queries)
        grad_key_w = grad_key_w + outer_sum(first_rows, grad_keys)
        grad_value_w = grad_value_w + outer_sum(first_rows, grad_values)
        grad_first = (
            times_transpose(grad_queries, w_query)
            + times_transpose(grad_keys, w_key)
            + times_transpose(grad_values, w_value)
        )
        grad_gain_attn = grad_gain_attn + jnp.sum(grad_first * normed_attn, axis=0)
        input_grads.append(
            grad_middle + norm_backward(grad_first * gain_attn, normed_attn, scale_attn)
        )
    shard_parts = halving_sum(
        (
            grad_query_w.reshape(-1),
            grad_key_w.reshape(-1),
            grad_value_w.reshape(-1),
            grad_out_w.reshape(-1),
            grad_gate_w.reshape(-1),
            grad_up_w.reshape(-1),
            grad_down_w.reshape(-1),
        ),
        lambda sent, bit: from_partner(sent, "seq", bit),
    )
    gain_sums = lax.psum((grad_gain_attn, grad_gain_mlp), "seq")
    return (
        jnp.stack(outputs),
        jnp.stack(input_grads),
        gain_sums[0],
        gain_sums[1],
        shard_parts[0],
        shard_parts[1],
        shard_parts[2],
        shard_parts[3],
        shard_parts[4],
        shard_parts[5],
        shard_parts[6],
    )


def solution(mesh):
    return jax.shard_map(
        per_device,
        mesh=mesh,
        in_specs=(
            P(None, "seq", None),
            P(),
            P(),
            P(),
            P(),
            P(),
            P(),
            P(),
            P(),
            P(),
            P(None, "seq", None),
            P(),
        ),
        out_specs=(
            P(None, "seq", None),
            P(None, "seq", None),
            P(),
            P(),
            P("seq"),
            P("seq"),
            P("seq"),
            P("seq"),
            P("seq"),
            P("seq"),
            P("seq"),
        ),
        check_vma=False,
    )
```

profile of v0, /device:TPU:0, one launch (start us, length us, event | category | flops | bytes accessed | tf_op | source)
XLA Modules:
  0.0 1954.1 jit_solution(12515243616024221602)
XLA Ops:
  212.9 5.9 fusion.294
  218.8 5.8 fusion.295
  224.6 5.9 fusion.299
  230.5 6.0 fusion.297
  243.5 5.9 fusion.162
  251.2 5.8 fusion.170
  258.8 5.8 fusion.166
  286.6 16.6 add_add_fusion.1
  303.3 16.3 add_add_fusion
  319.6 16.6 add_bitcast_fusion
  344.8 12.0 copy.145
  356.8 14.4 reshape.1494
  371.2 12.0 copy.146
  383.1 14.3 reshape.1495
  408.1 11.2 copy.183
  437.9 12.2 collective-permute-start.16
  477.6 900.5 %all-reduce.16 = (f32[1024]{0:T(1024)}, f32[1024]{0:T(1024)}) all-reduce(f32[1024]{0:T(1024)S(1)} %add_add_fusion.11, f32[1024]{0:T(1024)S(1)} %add_add_fusion.10), channel_id=1, replica_groups=mesh['seq'=32] {'seq'}, use_global_device_ids=true, to_apply=%region_40.41 | all-reduce | flops 2048 | bytes 16384 | tf_op jit(solution)/shard_map/psum | solution.py:260
  1388.8 130.4 %collective-permute-done.21 = f32[524288]{0:T(1024)S(1)} collective-permute-done((f32[524288]{0:T(1024)}, f32[524288]{0:T(1024)S(1)}, u32[]{:S(2)}, u32[]{:S(2)}) %collective-permute-start.21) | collective-permute-done | bytes 2097184 | tf_op jit(solution)/shard_map/ppermute | solution.py:23
  1519.4 44.7 %collective-permute-done.26 = f32[524288]{0:T(1024)S(1)} collective-permute-done((f32[524288]{0:T(1024)S(1)}, f32[524288]{0:T(1024)S(1)}, u32[]{:S(2)}, u32[]{:S(2)}) %collective-permute-start.26) | collective-permute-done | bytes 2097184 | tf_op jit(solution)/shard_map/ppermute | solution.py:23
  1564.6 22.0 %collective-permute-done.17 = f32[262144]{0:T(1024)S(1)} collective-permute-done((f32[262144]{0:T(1024)S(1)}, f32[262144]{0:T(1024)S(1)}, u32[]{:S(2)}, u32[]{:S(2)}) %collective-permute-start.17) | collective-permute-done | bytes 1048608 | tf_op jit(solution)/shard_map/ppermute | solution.py:23
  1586.7 22.4 %collective-permute-done.32 = f32[262144]{0:T(1024)S(1)} collective-permute-done((f32[262144]{0:T(1024)S(1)}, f32[262144]{0:T(1024)S(1)}, u32[]{:S(2)}, u32[]{:S(2)}) %collective-permute-start.32) | collective-permute-done | bytes 1048608 | tf_op jit(solution)/shard_map/ppermute | solution.py:23
  1609.3 22.3 %collective-permute-done.22 = f32[262144]{0:T(1024)S(1)} collective-permute-done((f32[262144]{0:T(1024)S(1)}, f32[262144]{0:T(1024)S(1)}, u32[]{:S(2)}, u32[]{:S(2)}) %collective-permute-start.22) | collective-permute-done | bytes 1048608 | tf_op jit(solution)/shard_map/ppermute | solution.py:23
  1633.0 20.9 %collective-permute-done.27 = f32[262144]{0:T(1024)S(1)} collective-permute-done((f32[262144]{0:T(1024)S(1)}, f32[262144]{0:T(1024)S(1)}, u32[]{:S(2)}, u32[]{:S(2)}) %collective-permute-start.27) | collective-permute-done | bytes 1048608 | tf_op jit(solution)/shard_map/ppermute | solution.py:23
  1656.3 12.4 collective-permute-done.33
  1670.2 9.8 collective-permute-done.23
  1681.4 8.9 collective-permute-done.28
  1692.5 7.0 collective-permute-done.34
  1728.9 52.4 %collective-permute-done.37 = f32[704512]{0:T(1024)S(1)} collective-permute-done((f32[704512]{0:T(1024)}, f32[704512]{0:T(1024)S(1)}, u32[]{:S(2)}, u32[]{:S(2)}) %collective-permute-start.37) | collective-permute-done | bytes 2818080 | tf_op jit(solution)/shard_map/ppermute | solution.py:23
  1783.2 58.6 %collective-permute-done.42 = f32[704512]{0:T(1024)S(1)} collective-permute-done((f32[704512]{0:T(1024)}, f32[704512]{0:T(1024)S(1)}, u32[]{:S(2)}, u32[]{:S(2)}) %collective-permute-start.42) | collective-permute-done | bytes 2818080 | tf_op jit(solution)/shard_map/ppermute | solution.py:23
  1843.6 58.1 %collective-permute-done.47 = f32[704512]{0:T(1024)S(1)} collective-permute-done((f32[704512]{0:T(1024)S(1)}, f32[704512]{0:T(1024)S(1)}, u32[]{:S(2)}, u32[]{:S(2)}) %collective-permute-start.47) | collective-permute-done | bytes 2818080 | tf_op jit(solution)/shard_map/ppermute | solution.py:23
  1906.1 28.5 %collective-permute-done.48 = f32[352256]{0:T(1024)S(1)} collective-permute-done((f32[352256]{0:T(1024)S(1)}, f32[352256]{0:T(1024)S(1)}, u32[]{:S(2)}, u32[]{:S(2)}) %collective-permute-start.48) | collective-permute-done | bytes 1409056 | tf_op jit(solution)/shard_map/ppermute | solution.py:23
  1937.1 14.2 collective-permute-done.49
  (746 shorter events, 370.7 us)
Async XLA Ops:
  4.5 57.4 %collective-permute-start.7 = (bf16[64,1024]{1,0:T(8,128)(2,1)S(1)}, bf16[64,1024]{1,0:T(8,128)(2,1)}, u32[]{:S(2)}, u32[]{:S(2)}) collective-permute-start(bf16[64,1024]{1,0:T(8,128)(2,1)S(1)} %convolution_convert_fusion.12), channel_id=1, source_target_pairs={{0,1},{1,2},{2,3},{3,4},{4,5},{5,6},{6,7},{7,8},{8,9},{9,10},{10,1... | collective-permute-start | bytes 393224 | tf_op jit(solution)/shard_map/ppermute | solution.py:19
  9.6 60.0 %collective-permute-start.6 = (bf16[64,1024]{1,0:T(8,128)(2,1)}, bf16[64,1024]{1,0:T(8,128)(2,1)}, u32[]{:S(2)}, u32[]{:S(2)}) collective-permute-start(bf16[64,1024]{1,0:T(8,128)(2,1)} %convolution_convert_fusion.14), channel_id=1, source_target_pairs={{0,1},{1,2},{2,3},{3,4},{4,5},{5,6},{6,7},{7,8},{8,9},{9,10},{10,1... | collective-permute-start | bytes 393224 | tf_op jit(solution)/shard_map/ppermute | solution.py:19
  15.4 63.7 %collective-permute-start.5 = (bf16[64,1024]{1,0:T(8,128)(2,1)}, bf16[64,1024]{1,0:T(8,128)(2,1)}, u32[]{:S(2)}, u32[]{:S(2)}) collective-permute-start(bf16[64,1024]{1,0:T(8,128)(2,1)} %convolution_convert_fusion.15), channel_id=1, source_target_pairs={{0,1},{1,2},{2,3},{3,4},{4,5},{5,6},{6,7},{7,8},{8,9},{9,10},{10,1... | collective-permute-start | bytes 393224 | tf_op jit(solution)/shard_map/ppermute | solution.py:19
  18.5 69.7 %collective-permute-start.4 = (bf16[64,1024]{1,0:T(8,128)(2,1)}, bf16[64,1024]{1,0:T(8,128)(2,1)}, u32[]{:S(2)}, u32[]{:S(2)}) collective-permute-start(bf16[64,1024]{1,0:T(8,128)(2,1)} %convolution_convert_fusion.17), channel_id=1, source_target_pairs={{0,1},{1,2},{2,3},{3,4},{4,5},{5,6},{6,7},{7,8},{8,9},{9,10},{10,1... | collective-permute-start | bytes 393224 | tf_op jit(solution)/shard_map/ppermute | solution.py:19
  23.2 71.4 %collective-permute-start.3 = (bf16[64,1024]{1,0:T(8,128)(2,1)}, bf16[64,1024]{1,0:T(8,128)(2,1)}, u32[]{:S(2)}, u32[]{:S(2)}) collective-permute-start(bf16[64,1024]{1,0:T(8,128)(2,1)} %convolution_convert_fusion.18), channel_id=1, source_target_pairs={{0,1},{1,2},{2,3},{3,4},{4,5},{5,6},{6,7},{7,8},{8,9},{9,10},{10,1... | collective-permute-start | bytes 393224 | tf_op jit(solution)/shard_map/ppermute | solution.py:19
  61.9 37.0 %collective-permute-start.2 = (bf16[64,1024]{1,0:T(8,128)(2,1)}, bf16[64,1024]{1,0:T(8,128)(2,1)}, u32[]{:S(2)}, u32[]{:S(2)}) collective-permute-start(bf16[64,1024]{1,0:T(8,128)(2,1)} %convolution_convert_fusion.20), channel_id=1, source_target_pairs={{0,1},{1,2},{2,3},{3,4},{4,5},{5,6},{6,7},{7,8},{8,9},{9,10},{10,1... | collective-permute-start | bytes 393224 | tf_op jit(solution)/shard_map/ppermute | solution.py:19
  69.6 37.4 %collective-permute-start.1 = (bf16[64,1024]{1,0:T(8,128)(2,1)S(1)}, bf16[64,1024]{1,0:T(8,128)(2,1)}, u32[]{:S(2)}, u32[]{:S(2)}) collective-permute-start(bf16[64,1024]{1,0:T(8,128)(2,1)S(1)} %convolution_convert_fusion.21), channel_id=1, source_target_pairs={{0,1},{1,2},{2,3},{3,4},{4,5},{5,6},{6,7},{7,8},{8,9},{9,10},{10,1... | collective-permute-start | bytes 393224 | tf_op jit(solution)/shard_map/ppermute | solution.py:19
  79.1 33.1 %collective-permute-start = (bf16[64,1024]{1,0:T(8,128)(2,1)}, bf16[64,1024]{1,0:T(8,128)(2,1)}, u32[]{:S(2)}, u32[]{:S(2)}) collective-permute-start(bf16[64,1024]{1,0:T(8,128)(2,1)} %convolution_convert_fusion.23), channel_id=1, source_target_pairs={{0,1},{1,2},{2,3},{3,4},{4,5},{5,6},{6,7},{7,8},{8,9},{9,10},{10,1... | collective-permute-start | bytes 393224 | tf_op jit(solution)/shard_map/ppermute | solution.py:19
  267.5 157.5 %collective-permute-start.8 = (bf16[64,1024]{0,1:T(8,128)(2,1)}, bf16[64,1024]{0,1:T(8,128)(2,1)}, u32[]{:S(2)}, u32[]{:S(2)}) collective-permute-start(bf16[64,1024]{0,1:T(8,128)(2,1)} %fusion.30), channel_id=1, source_target_pairs={{1,0},{2,1},{3,2},{4,3},{5,4},{6,5},{7,6},{8,7},{9,8},{10,9},{11,1... | collective-permute-start | bytes 393224 | tf_op jit(solution)/shard_map/ppermute | solution.py:19
  269.9 159.3 %collective-permute-start.9 = (bf16[64,1024]{0,1:T(8,128)(2,1)}, bf16[64,1024]{0,1:T(8,128)(2,1)}, u32[]{:S(2)}, u32[]{:S(2)}) collective-permute-start(bf16[64,1024]{0,1:T(8,128)(2,1)} %fusion.28), channel_id=1, source_target_pairs={{1,0},{2,1},{3,2},{4,3},{5,4},{6,5},{7,6},{8,7},{9,8},{10,9},{11,1... | collective-permute-start | bytes 393224 | tf_op jit(solution)/shard_map/ppermute | solution.py:19
  272.4 161.2 %collective-permute-start.10 = (bf16[64,1024]{0,1:T(8,128)(2,1)}, bf16[64,1024]{0,1:T(8,128)(2,1)}, u32[]{:S(2)}, u32[]{:S(2)}) collective-permute-start(bf16[64,1024]{0,1:T(8,128)(2,1)} %fusion.26), channel_id=1, source_target_pairs={{1,0},{2,1},{3,2},{4,3},{5,4},{6,5},{7,6},{8,7},{9,8},{10,9},{11,1... | collective-permute-start | bytes 393224 | tf_op jit(solution)/shard_map/ppermute | solution.py:19
  275.1 162.8 %collective-permute-start.11 = (bf16[64,1024]{0,1:T(8,128)(2,1)}, bf16[64,1024]{0,1:T(8,128)(2,1)}, u32[]{:S(2)}, u32[]{:S(2)}) collective-permute-start(bf16[64,1024]{0,1:T(8,128)(2,1)} %fusion.24), channel_id=1, source_target_pairs={{1,0},{2,1},{3,2},{4,3},{5,4},{6,5},{7,6},{8,7},{9,8},{10,9},{11,1... | collective-permute-start | bytes 393224 | tf_op jit(solution)/shard_map/ppermute | solution.py:19
  277.7 175.3 %collective-permute-start.12 = (bf16[64,1024]{0,1:T(8,128)(2,1)}, bf16[64,1024]{0,1:T(8,128)(2,1)}, u32[]{:S(2)}, u32[]{:S(2)}) collective-permute-start(bf16[64,1024]{0,1:T(8,128)(2,1)} %fusion.22), channel_id=1, source_target_pairs={{1,0},{2,1},{3,2},{4,3},{5,4},{6,5},{7,6},{8,7},{9,8},{10,9},{11,1... | collective-permute-start | bytes 393224 | tf_op jit(solution)/shard_map/ppermute | solution.py:19
  433.6 34.1 %collective-permute-start.15 = (bf16[64,1024]{0,1:T(8,128)(2,1)S(1)}, bf16[64,1024]{0,1:T(8,128)(2,1)S(1)}, u32[]{:S(2)}, u32[]{:S(2)}) collective-permute-start(bf16[64,1024]{0,1:T(8,128)(2,1)S(1)} %copy-done.144), channel_id=1, source_target_pairs={{1,0},{2,1},{3,2},{4,3},{5,4},{6,5},{7,6},{8,7},{9,8},{10,9},{11,1... | collective-permute-start | bytes 393224 | tf_op jit(solution)/shard_map/ppermute | solution.py:19
  437.9 944.0 %collective-permute-start.16 = (f32[524288]{0:T(1024)}, f32[524288]{0:T(1024)}, u32[]{:S(2)}, u32[]{:S(2)}) collective-permute-start(f32[524288]{0:T(1024)} %dynamic_slice.211), channel_id=1, source_target_pairs={{0,16},{1,17},{2,18},{3,19},{4,20},{5,21},{6,22},{7,23},{8,24},{9,... | collective-permute-start | bytes 6291464 | tf_op jit(solution)/shard_map/ppermute | solution.py:23
  452.9 931.6 %collective-permute-start.31 = (f32[524288]{0:T(1024)}, f32[524288]{0:T(1024)}, u32[]{:S(2)}, u32[]{:S(2)}) collective-permute-start(f32[524288]{0:T(1024)} %dynamic_slice.241), channel_id=1, source_target_pairs={{0,16},{1,17},{2,18},{3,19},{4,20},{5,21},{6,22},{7,23},{8,24},{9,... | collective-permute-start | bytes 6291464 | tf_op jit(solution)/shard_map/ppermute | solution.py:23
  456.1 1256.3 %collective-permute-start.36 = (f32[1409024]{0:T(1024)}, f32[1409024]{0:T(1024)}, u32[]{:S(2)}, u32[]{:S(2)}) collective-permute-start(f32[1409024]{0:T(1024)} %dynamic_slice.251), channel_id=1, source_target_pairs={{0,16},{1,17},{2,18},{3,19},{4,20},{5,21},{6,22},{7,23},{8,24},{9,... | collective-permute-start | bytes 16908296 | tf_op jit(solution)/shard_map/ppermute | solution.py:23
  460.6 1256.6 %collective-permute-start.41 = (f32[1409024]{0:T(1024)}, f32[1409024]{0:T(1024)}, u32[]{:S(2)}, u32[]{:S(2)}) collective-permute-start(f32[1409024]{0:T(1024)} %dynamic_slice.261), channel_id=1, source_target_pairs={{0,16},{1,17},{2,18},{3,19},{4,20},{5,21},{6,22},{7,23},{8,24},{9,... | collective-permute-start | bytes 16908296 | tf_op jit(solution)/shard_map/ppermute | solution.py:23
  467.7 1257.0 %collective-permute-start.46 = (f32[1409024]{0:T(1024)}, f32[1409024]{0:T(1024)}, u32[]{:S(2)}, u32[]{:S(2)}) collective-permute-start(f32[1409024]{0:T(1024)} %dynamic_slice.271), channel_id=1, source_target_pairs={{0,16},{1,17},{2,18},{3,19},{4,20},{5,21},{6,22},{7,23},{8,24},{9,... | collective-permute-start | bytes 16908296 | tf_op jit(solution)/shard_map/ppermute | solution.py:23
  1381.9 137.3 %collective-permute-start.21 = (f32[524288]{0:T(1024)}, f32[524288]{0:T(1024)S(1)}, u32[]{:S(2)}, u32[]{:S(2)}) collective-permute-start(f32[524288]{0:T(1024)} %dynamic_slice.221), channel_id=1, source_target_pairs={{0,16},{1,17},{2,18},{3,19},{4,20},{5,21},{6,22},{7,23},{8,24},{9,... | collective-permute-start | bytes 6291464 | tf_op jit(solution)/shard_map/ppermute | solution.py:23
  1384.6 179.6 %collective-permute-start.26 = (f32[524288]{0:T(1024)S(1)}, f32[524288]{0:T(1024)S(1)}, u32[]{:S(2)}, u32[]{:S(2)}) collective-permute-start(f32[524288]{0:T(1024)S(1)} %copy-done.102), channel_id=1, source_target_pairs={{0,16},{1,17},{2,18},{3,19},{4,20},{5,21},{6,22},{7,23},{8,24},{9,... | collective-permute-start | bytes 6291464 | tf_op jit(solution)/shard_map/ppermute | solution.py:23
  1519.2 67.4 %collective-permute-start.17 = (f32[262144]{0:T(1024)S(1)}, f32[262144]{0:T(1024)S(1)}, u32[]{:S(2)}, u32[]{:S(2)}) collective-permute-start(f32[262144]{0:T(1024)S(1)} %dynamic_slice.213), channel_id=1, source_target_pairs={{0,8},{1,9},{2,10},{3,11},{4,12},{5,13},{6,14},{7,15},{8,0},{9,1},... | collective-permute-start | bytes 3145736 | tf_op jit(solution)/shard_map/ppermute | solution.py:23
  1564.2 44.9 %collective-permute-start.32 = (f32[262144]{0:T(1024)S(1)}, f32[262144]{0:T(1024)S(1)}, u32[]{:S(2)}, u32[]{:S(2)}) collective-permute-start(f32[262144]{0:T(1024)S(1)} %dynamic_slice.243), channel_id=1, source_target_pairs={{0,8},{1,9},{2,10},{3,11},{4,12},{5,13},{6,14},{7,15},{8,0},{9,1},... | collective-permute-start | bytes 3145736 | tf_op jit(solution)/shard_map/ppermute | solution.py:23
  1586.6 44.9 %collective-permute-start.22 = (f32[262144]{0:T(1024)S(1)}, f32[262144]{0:T(1024)S(1)}, u32[]{:S(2)}, u32[]{:S(2)}) collective-permute-start(f32[262144]{0:T(1024)S(1)} %dynamic_slice.223), channel_id=1, source_target_pairs={{0,8},{1,9},{2,10},{3,11},{4,12},{5,13},{6,14},{7,15},{8,0},{9,1},... | collective-permute-start | bytes 3145736 | tf_op jit(solution)/shard_map/ppermute | solution.py:23
  1609.1 44.8 %collective-permute-start.27 = (f32[262144]{0:T(1024)S(1)}, f32[262144]{0:T(1024)S(1)}, u32[]{:S(2)}, u32[]{:S(2)}) collective-permute-start(f32[262144]{0:T(1024)S(1)} %dynamic_slice.233), channel_id=1, source_target_pairs={{0,8},{1,9},{2,10},{3,11},{4,12},{5,13},{6,14},{7,15},{8,0},{9,1},... | collective-permute-start | bytes 3145736 | tf_op jit(solution)/shard_map/ppermute | solution.py:23
  1717.3 64.1 %collective-permute-start.37 = (f32[704512]{0:T(1024)}, f32[704512]{0:T(1024)S(1)}, u32[]{:S(2)}, u32[]{:S(2)}) collective-permute-start(f32[704512]{0:T(1024)} %dynamic_slice.253), channel_id=1, source_target_pairs={{0,8},{1,9},{2,10},{3,11},{4,12},{5,13},{6,14},{7,15},{8,0},{9,1},... | collective-permute-start | bytes 8454152 | tf_op jit(solution)/shard_map/ppermute | solution.py:23
  1723.6 118.1 %collective-permute-start.42 = (f32[704512]{0:T(1024)}, f32[704512]{0:T(1024)S(1)}, u32[]{:S(2)}, u32[]{:S(2)}) collective-permute-start(f32[704512]{0:T(1024)} %dynamic_slice.263), channel_id=1, source_target_pairs={{0,8},{1,9},{2,10},{3,11},{4,12},{5,13},{6,14},{7,15},{8,0},{9,1},... | collective-permute-start | bytes 8454152 | tf_op jit(solution)/shard_map/ppermute | solution.py:23
  1727.9 173.8 %collective-permute-start.47 = (f32[704512]{0:T(1024)S(1)}, f32[704512]{0:T(1024)S(1)}, u32[]{:S(2)}, u32[]{:S(2)}) collective-permute-start(f32[704512]{0:T(1024)S(1)} %dynamic_slice.273), channel_id=1, source_target_pairs={{0,8},{1,9},{2,10},{3,11},{4,12},{5,13},{6,14},{7,15},{8,0},{9,1},... | collective-permute-start | bytes 8454152 | tf_op jit(solution)/shard_map/ppermute | solution.py:23
  1781.8 121.7 %collective-permute-start.38 = (f32[352256]{0:T(1024)S(1)}, f32[352256]{0:T(1024)S(1)}, u32[]{:S(2)}, u32[]{:S(2)}) collective-permute-start(f32[352256]{0:T(1024)S(1)} %dynamic_slice.255), channel_id=1, source_target_pairs={{0,4},{1,5},{2,6},{3,7},{4,0},{5,1},{6,2},{7,3},{8,12},{9,13},{10,... | collective-permute-start | bytes 4227080 | tf_op jit(solution)/shard_map/ppermute | solution.py:23
  1842.2 63.1 %collective-permute-start.43 = (f32[352256]{0:T(1024)S(1)}, f32[352256]{0:T(1024)S(1)}, u32[]{:S(2)}, u32[]{:S(2)}) collective-permute-start(f32[352256]{0:T(1024)S(1)} %dynamic_slice.265), channel_id=1, source_target_pairs={{0,4},{1,5},{2,6},{3,7},{4,0},{5,1},{6,2},{7,3},{8,12},{9,13},{10,... | collective-permute-start | bytes 4227080 | tf_op jit(solution)/shard_map/ppermute | solution.py:23
  1902.1 32.5 %collective-permute-start.48 = (f32[352256]{0:T(1024)S(1)}, f32[352256]{0:T(1024)S(1)}, u32[]{:S(2)}, u32[]{:S(2)}) collective-permute-start(f32[352256]{0:T(1024)S(1)} %dynamic_slice.275), channel_id=1, source_target_pairs={{0,4},{1,5},{2,6},{3,7},{4,0},{5,1},{6,2},{7,3},{8,12},{9,13},{10,... | collective-permute-start | bytes 4227080 | tf_op jit(solution)/shard_map/ppermute | solution.py:23
  1903.7 32.5 %collective-permute-start.39 = (f32[176128]{0:T(1024)S(1)}, f32[176128]{0:T(1024)S(1)}, u32[]{:S(2)}, u32[]{:S(2)}) collective-permute-start(f32[176128]{0:T(1024)S(1)} %dynamic_slice.257), channel_id=1, source_target_pairs={{0,2},{1,3},{2,0},{3,1},{4,6},{5,7},{6,4},{7,5},{8,10},{9,11},{10,... | collective-permute-start | bytes 2113544 | tf_op jit(solution)/shard_map/ppermute | solution.py:23
  (209 other events, 3874.4 us)
where the time goes:
time: 1960 us; the launch traced here: 1950 us
  blocking collectives  900 us (46%)
  waiting for transfers between devices  520 us (27%)
  matrix products  252 us (13%)
  local copies, waits for them, and re-layouts  140 us (7%)
  starting transfers between devices  76.3 us (4%)
  other arithmetic  60.7 us (3%)
    psum x1, blocking collectives, per_device(): gain_sums = lax.psum((grad_gain_attn, grad_gain_mlp), 'seq')  900 us
    ppermute x35, waiting for transfers between devices, from_partner(): lax.ppermute(value, axis, [(i, i ^ 1 << bit) for i in range(lax.axis_size...  520 us
    dot_general x28, matrix products, outer_sum(): lax.dot_general(left, right, (((0,), (0,)), ((), ())), preferred_element_...  117 us
    ppermute x35, starting transfers between devices, from_partner(): lax.ppermute(value, axis, [(i, i ^ 1 << bit) for i in range(lax.axis_size...  41.2 us
    dot_general x28, matrix products, times_transpose(): lax.dot_general(left, weight, (((1,), (1,)), ((), ())), preferred_element...  40.1 us
  transfers between devices with their start and end apart: 51, of which 18 were waited for; matrix products, arithmetic and copies ran while one was open for 14% of the time, Pallas kernels for 0%

commit v1 on v0

v1 whole, which is shorter than its diff:
```python
import functools
import math

import jax
import jax.numpy as jnp
from jax import lax
from jax.experimental import pallas as pl
from jax.experimental.pallas import tpu as pltpu
from jax.sharding import PartitionSpec as P

HEAD = 64
WIN = 64
EPSILON = 1e-05
LOGICAL = pl.DeviceIdType.MESH
MOST_GROUPS = 32
BF16 = jnp.bfloat16
F32 = jnp.float32


def round_up(value, unit):
    return -(-value // unit) * unit


ROW_FACTORS = ("hidden", "second", "first", "attended")
MATRICES = (
    ("down", "hidden", "cot"),
    ("gate", "second", "dgate"),
    ("up", "second", "dup"),
    ("query", "first", "dquery"),
    ("keyval", "first", "dkeyval"),
    ("out", "attended", "branch"),
)


def bit_orders(bits):
    ascending = list(range(1, bits + 1))
    swapped = [2, 1] + ascending[2:]
    last_first = ascending[2:] + [1, 2]
    return {
        "down": last_first,
        "gate": ascending,
        "query": ascending,
        "out": ascending,
        "up": swapped,
        "keyval": swapped,
    }


def bit_of(number, bit):
    return (number // (1 << bit)) % 2


def flip(number, bit):
    return number + (1 << bit) * (1 - 2 * bit_of(number, bit))


def reduce_kernel(bits, lower, names, *refs):
    count = 1 << bits
    half = count // 2
    orders = bit_orders(bits)
    refs = list(refs)

    def take(how_many):
        taken = refs[:how_many]
        del refs[:how_many]
        return taken

    row_names = [name for name in ROW_FACTORS]
    col_names = [col for _, _, col in MATRICES]
    row_in = dict(zip(row_names, take(len(row_names))))
    col_in = dict(zip(col_names, take(len(col_names))))
    (gains_in,) = take(1)
    outs = dict(zip(names, take(len(names))))
    (gains_out,) = take(1)
    rows = dict(zip(row_names, take(len(row_names))))
    cols = dict(zip(col_names, take(len(col_names))))
    send_buf = dict(zip(names, take(len(names))))
    own_buf = dict(zip(names, take(len(names))))
    landed = {name: take(bits) for name in names}
    (gain_buf, local_sem, pair_send, pair_recv, step_send, step_recv, gain_send, gain_recv) = refs

    position = lax.axis_index("seq")
    me, rest = position // lower, position % lower
    core = me % 2
    my_unit = me // 2

    def partner(bit):
        return (flip(me, bit) * lower + rest,)

    def unit_at(order, slot):
        unit = my_unit
        for place, bit in enumerate(order):
            rel = (slot // (1 << (bits - 1 - place))) % 2
            own = bit_of(me, bit)
            unit = unit + (1 << (bit - 1)) * rel * (1 - 2 * own)
        return unit

    barrier = pltpu.get_barrier_semaphore()
    for bit in range(bits + 1):
        pl.semaphore_signal(barrier, inc=1, device_id=partner(bit), device_id_type=LOGICAL)
    pl.semaphore_wait(barrier, bits + 1)

    factor_copies = {}
    for index, (kind, name) in enumerate(
        [("row", "hidden"), ("col", "cot"), ("row", "second"), ("col", "dgate"), ("col", "dup"),
         ("row", "first"), ("col", "dquery"), ("col", "dkeyval"), ("row", "attended"), ("col", "branch")]
    ):
        if kind == "row":
            mine, theirs, kept = row_in[name].at[core], row_in[name].at[1 - core], rows[name]
        else:
            mine, theirs, kept = col_in[name], col_in[name], cols[name]
        local = pltpu.make_async_copy(mine, kept.at[0], local_sem.at[index])
        remote = pltpu.make_async_remote_copy(
            src_ref=theirs, dst_ref=kept.at[1], send_sem=pair_send.at[index], recv_sem=pair_recv.at[index],
            device_id=partner(0), device_id_type=LOGICAL,
        )
        local.start()
        remote.start()
        factor_copies[name] = (local, remote)
    ready = set()

    def need(name):
        if name not in ready:
            ready.add(name)
            local, remote = factor_copies[name]
            local.wait()
            remote.wait_recv()

    def product(index, into, base):
        name, row_name, col_name = MATRICES[index]
        need(row_name)
        need(col_name)
        order = orders[name]
        row_ref, col_ref = rows[row_name], cols[col_name]
        unit_rows = row_ref.shape[2]
        width = col_ref.shape[2]
        step = 256
        units = [unit_at(order, base + slot) for slot in range(half)]
        lefts = [
            jnp.concatenate([row_ref[source, unit] for unit in units], axis=0) for source in range(2)
        ]

        def body(at, carry):
            lanes = pl.ds(pl.multiple_of(at * step, step), step)
            total = jnp.dot(lefts[0], col_ref[0, :, lanes], preferred_element_type=F32)
            total += jnp.dot(lefts[1], col_ref[1, :, lanes], preferred_element_type=F32)
            into[:, :, lanes] = total.astype(BF16).reshape(half, unit_rows, step)
            return carry

        lax.fori_loop(0, width // step, body, 0)

    def step_copy(index, level, slot):
        name = MATRICES[index][0]
        bit = orders[name][level]
        size = half >> level
        source = send_buf[name].at[slot] if level == 0 else landed[name][level - 1].at[size + slot]
        place = count - 2 * size + slot
        return pltpu.make_async_remote_copy(
            src_ref=source, dst_ref=landed[name][level].at[slot],
            send_sem=step_send.at[index, place], recv_sem=step_recv.at[index, place],
            device_id=partner(bit), device_id_type=LOGICAL,
        )

    def start_level_zero(index):
        def body(at, carry):
            step_copy(index, 0, (at + half // 2) % half).start()
            return carry

        lax.fori_loop(0, half, body, 0)

    def arrive(index, level, first, last, forward):
        name = MATRICES[index][0]
        size = half >> level
        buffer = landed[name][level]
        before = own_buf[name] if level == 0 else landed[name][level - 1]

        def body(slot, carry):
            step_copy(index, level, slot).wait_recv()
            total = buffer[slot].astype(F32) + before[slot].astype(F32)
            if level == bits - 1:
                outs[name][...] = total
            else:
                buffer[slot] = total.astype(BF16)
            if forward:
                step_copy(index, level + 1, slot - size // 2).start()
            return carry

        lax.fori_loop(first, last, body, 0)

    for index in range(len(MATRICES)):
        product(index, send_buf[MATRICES[index][0]], half)
        start_level_zero(index)
    for index in range(len(MATRICES)):
        product(index, own_buf[MATRICES[index][0]], 0)

    gain_buf[0] = gains_in[...]

    def gain_copy(bit):
        return pltpu.make_async_remote_copy(
            src_ref=gain_buf.at[2 * bit], dst_ref=gain_buf.at[2 * bit + 1],
            send_sem=gain_send.at[bit], recv_sem=gain_recv.at[bit],
            device_id=partner(bit), device_id_type=LOGICAL,
        )

    def gain_step(bit):
        gain_copy(bit).wait_recv()
        total = gain_buf[2 * bit] + gain_buf[2 * bit + 1]
        if bit < bits:
            gain_buf[2 * bit + 2] = total
            gain_copy(bit + 1).start()
        else:
            gains_out[...] = total

    gain_copy(0).start()
    index_of = {name: index for index, (name, _, _) in enumerate(MATRICES)}
    turn = [index_of[name] for name in ("gate", "up", "down", "query", "keyval", "out")]
    for level in range(bits):
        size = half >> level
        gain_step(level)
        for index in turn:
            if size > 1:
                arrive(index, level, size // 2, size, True)
        for index in turn:
            arrive(index, level, 0, max(size // 2, 1), False)
    gain_step(bits)

    for local, remote in factor_copies.values():
        remote.wait_send()
    for bit in range(bits + 1):
        gain_copy(bit).wait_send()
    for index in range(len(MATRICES)):
        for level in range(bits):

            def drain(slot, carry, index=index, level=level):
                step_copy(index, level, slot).wait_send()
                return carry

            lax.fori_loop(0, half >> level, drain, 0)


def reduce_scatter(row_factors, col_factors, gains, bits, lower):
    count = 1 << bits
    half = count // 2
    names = tuple(name for name, _, _ in MATRICES)
    any_spec = pl.BlockSpec(memory_space=pl.ANY)
    vmem_spec = pl.BlockSpec(memory_space=pltpu.VMEM)
    row_args = [row_factors[name] for name in ROW_FACTORS]
    col_args = [col_factors[col] for _, _, col in MATRICES]
    shapes = {
        name: (row_factors[row].shape[2], col_factors[col].shape[1]) for name, row, col in MATRICES
    }
    scratch = [pltpu.VMEM((2,) + row.shape[1:], BF16) for row in row_args]
    scratch += [pltpu.VMEM((2,) + col.shape, BF16) for col in col_args]
    scratch += [pltpu.VMEM((half,) + shapes[name], BF16) for name in names]
    scratch += [pltpu.VMEM((half,) + shapes[name], BF16) for name in names]
    for name in names:
        scratch += [pltpu.VMEM((half >> level,) + shapes[name], BF16) for level in range(bits)]
    factors = len(row_args) + len(col_args)
    scratch += [
        pltpu.VMEM((2 * bits + 2,) + gains.shape, F32),
        pltpu.SemaphoreType.DMA((factors,)),
        pltpu.SemaphoreType.DMA((factors,)),
        pltpu.SemaphoreType.DMA((factors,)),
        pltpu.SemaphoreType.DMA((len(names), count)),
        pltpu.SemaphoreType.DMA((len(names), count)),
        pltpu.SemaphoreType.DMA((bits + 1,)),
        pltpu.SemaphoreType.DMA((bits + 1,)),
    ]
    results = pl.pallas_call(
        functools.partial(reduce_kernel, bits, lower, names),
        out_shape=[jax.ShapeDtypeStruct(shapes[name], F32) for name in names]
        + [jax.ShapeDtypeStruct(gains.shape, F32)],
        in_specs=[any_spec] * factors + [vmem_spec],
        out_specs=[vmem_spec] * (len(names) + 1),
        scratch_shapes=scratch,
        compiler_params=pltpu.CompilerParams(
            collective_id=0, has_side_effects=True, vmem_limit_bytes=62 * 2**20
        ),
        name="weight_grads",
    )(*row_args, *col_args, gains)
    return dict(zip(names, results[:-1])), results[-1]


def times_transpose(left, weight):
    return lax.dot_general(left, weight, (((1,), (1,)), ((), ())), preferred_element_type=F32)


def norm_backward(grad_normed, normed, row_scale):
    return row_scale * (
        grad_normed - normed * jnp.mean(grad_normed * normed, axis=-1, keepdims=True)
    )


def shifted(value, steps):
    count = lax.axis_size("seq")
    leading, last = max(0, -steps), min(count, count - steps)
    return lax.ppermute(value, "seq", [(source, source + steps) for source in range(leading, last)])


def band_mask(lengths, start):
    ends = jnp.cumsum(lengths, axis=1)
    positions = start + jnp.arange(-WIN, WIN, dtype=jnp.int32)
    segments = jnp.sum((ends[:, None, :] <= positions[None, :, None]).astype(jnp.int32), axis=2)
    offset = positions[WIN:, None] - positions[None, :]
    near = (offset >= 0) & (offset < WIN) & (positions[None, :] >= 0)
    return near[None] & (segments[:, WIN:, None] == segments[:, None, :])


def per_device(
    tokens, gain_attn, gain_mlp, w_query, w_key, w_value, w_out, w_gate, w_up, w_down, cotangent, lengths
):
    devices = lax.axis_size("seq")
    groups = min(devices, MOST_GROUPS)
    lower = devices // groups
    bits = groups.bit_length() - 2
    micro, block, width = tokens.shape
    heads = width // HEAD
    rows_all = micro * block
    score_scale = 1.0 / math.sqrt(HEAD)
    start = lax.axis_index("seq") * block
    allowed = band_mask(lengths, start)[:, None]

    inputs = tokens.reshape(rows_all, width).astype(F32)
    scale_attn = lax.rsqrt(jnp.mean(inputs * inputs, axis=-1, keepdims=True) + EPSILON)
    normed_attn = inputs * scale_attn
    first = (normed_attn * gain_attn).astype(BF16)
    queries = jnp.dot(first, w_query, preferred_element_type=F32).astype(BF16)
    keys = jnp.dot(first, w_key, preferred_element_type=F32).astype(BF16)
    values = jnp.dot(first, w_value, preferred_element_type=F32).astype(BF16)
    before_keys, before_values = shifted((keys, values), 1)

    def joined(before, own):
        both = jnp.stack([before.reshape(micro, block, width), own.reshape(micro, block, width)], axis=1)
        return both.reshape(micro, 2 * block, heads, HEAD)

    query_blocks = queries.reshape(micro, block, heads, HEAD)
    key_blocks = joined(before_keys, keys)
    value_blocks = joined(before_values, values)
    scores = jnp.einsum("bqhd,bkhd->bhqk", query_blocks, key_blocks, preferred_element_type=F32)
    logits = jnp.where(allowed, scores * score_scale, -1e30)
    exp_scores = jnp.exp(logits - jnp.max(logits, axis=-1, keepdims=True))
    probability = exp_scores / jnp.sum(exp_scores, axis=-1, keepdims=True)
    rounded = probability.astype(BF16)
    attended = jnp.einsum("bhqk,bkhd->bqhd", rounded, value_blocks, preferred_element_type=F32)
    attended = attended.reshape(rows_all, width).astype(BF16)
    middle = inputs + jnp.dot(attended, w_out, preferred_element_type=F32)
    scale_mlp = lax.rsqrt(jnp.mean(middle * middle, axis=-1, keepdims=True) + EPSILON)
    normed_mlp = middle * scale_mlp
    second = (normed_mlp * gain_mlp).astype(BF16)
    gate = jnp.dot(second, w_gate, preferred_element_type=F32)
    up = jnp.dot(second, w_up, preferred_element_type=F32)
    sigmoid = jax.nn.sigmoid(gate)
    silu = gate * sigmoid
    hidden = (silu * up).astype(BF16)
    output = (middle + jnp.dot(hidden, w_down, preferred_element_type=F32)).astype(BF16)

    cot = cotangent.reshape(rows_all, width)
    grad_hidden = times_transpose(cot, w_down)
    dgate = (grad_hidden * up * sigmoid * (1.0 + gate * (1.0 - sigmoid))).astype(BF16)
    dup = (grad_hidden * silu).astype(BF16)
    grad_second = times_transpose(dgate, w_gate) + times_transpose(dup, w_up)
    grad_gain_mlp = jnp.sum(grad_second * normed_mlp, axis=0)
    grad_middle = cot.astype(F32) + norm_backward(grad_second * gain_mlp, normed_mlp, scale_mlp)
    branch = grad_middle.astype(BF16)
    grad_attended = times_transpose(branch, w_out).astype(BF16).reshape(micro, block, heads, HEAD)
    grad_prob = jnp.einsum("bqhd,bkhd->bhqk", grad_attended, value_blocks, preferred_element_type=F32)
    delta = jnp.sum(probability * grad_prob, axis=-1, keepdims=True)
    grad_scores = (score_scale * probability * (grad_prob - delta)).astype(BF16)
    dquery = jnp.einsum("bhqk,bkhd->bqhd", grad_scores, key_blocks, preferred_element_type=F32)
    dquery = dquery.reshape(rows_all, width).astype(BF16)
    dkey_both = jnp.einsum("bhqk,bqhd->bkhd", grad_scores, query_blocks, preferred_element_type=F32)
    dvalue_both = jnp.einsum("bhqk,bqhd->bkhd", rounded, grad_attended, preferred_element_type=F32)

    def halves(both):
        both = both.reshape(micro, 2, block, width)
        return both[:, 0].reshape(rows_all, width).astype(BF16), both[:, 1].reshape(rows_all, width)

    key_back, key_own = halves(dkey_both)
    value_back, value_own = halves(dvalue_both)
    key_back, value_back = shifted((key_back, value_back), -1)
    dkey = (key_own + key_back.astype(F32)).astype(BF16)
    dvalue = (value_own + value_back.astype(F32)).astype(BF16)
    grad_first = (
        times_transpose(dquery, w_query) + times_transpose(dkey, w_key) + times_transpose(dvalue, w_value)
    )
    grad_gain_attn = jnp.sum(grad_first * normed_attn, axis=0)
    input_grad = grad_middle + norm_backward(grad_first * gain_attn, normed_attn, scale_attn)

    hidden_width = w_gate.shape[1]
    padded = round_up(hidden_width, 256)
    unit_rows = {"first": width // groups, "second": width // groups, "attended": width // groups}
    unit_rows["hidden"] = hidden_width // groups

    def by_owner(value, own_rows):
        parts = value.T.reshape(groups // 2, 2, own_rows, rows_all).transpose(1, 0, 2, 3)
        pad = round_up(own_rows, 16) - own_rows
        return jnp.pad(parts, ((0, 0), (0, 0), (0, pad), (0, 0)))

    def widened(value):
        return jnp.pad(value, ((0, 0), (0, padded - hidden_width)))

    row_factors = {
        "first": by_owner(first, unit_rows["first"]),
        "second": by_owner(second, unit_rows["second"]),
        "attended": by_owner(attended, unit_rows["attended"]),
        "hidden": by_owner(hidden, unit_rows["hidden"]),
    }
    col_factors = {
        "cot": cot,
        "dgate": widened(dgate),
        "dup": widened(dup),
        "dquery": dquery,
        "dkeyval": jnp.concatenate([dkey, dvalue], axis=1),
        "branch": branch,
    }
    gains = jnp.concatenate(
        [grad_gain_attn[None], grad_gain_mlp[None], jnp.zeros((6, width), F32)], axis=0
    )
    sums, gain_sums = reduce_scatter(row_factors, col_factors, gains, bits, lower)
    own = unit_rows["first"]

    def slice_of(value):
        flat = value.reshape(-1)
        if lower == 1:
            return flat
        near = [[high * lower + low for low in range(lower)] for high in range(groups)]
        return lax.psum_scatter(flat, "seq", axis_index_groups=near, tiled=True)

    if lower > 1:
        across = [[high * lower + low for low in range(lower)] for high in range(groups)]
        gain_sums = lax.psum(gain_sums, "seq", axis_index_groups=across)
    return (
        output.reshape(tokens.shape),
        input_grad.reshape(tokens.shape),
        gain_sums[0],
        gain_sums[1],
        slice_of(sums["query"][:own]),
        slice_of(sums["keyval"][:own, :width]),
        slice_of(sums["keyval"][:own, width:]),
        slice_of(sums["out"][:own]),
        slice_of(sums["gate"][:own, :hidden_width]),
        slice_of(sums["up"][:own, :hidden_width]),
        slice_of(sums["down"][: unit_rows["hidden"]]),
    )


def solution(mesh):
    tokens_spec = P(None, "seq", None)
    return jax.shard_map(
        per_device,
        mesh=mesh,
        in_specs=(tokens_spec,) + (P(),) * 9 + (tokens_spec, P()),
        out_specs=(tokens_spec, tokens_spec, P(), P()) + (P("seq"),) * 7,
        check_vma=False,
    )
```

time: 1960 us -> 335 us (0.17)
  blocking collectives: 900 us -> 0 us
  waiting for transfers between devices: 520 us -> 0.01 us
  matrix products: 252 us -> 58.4 us
  Pallas kernels: 0 us -> 136 us
  starting transfers between devices: 76.3 us -> 9.6 us
  other arithmetic: 60.7 us -> 14.3 us
  local copies, waits for them, and re-layouts: 140 us -> 111 us
    psum x1 -> x0, blocking collectives: 900 us -> none  [per_device(): gain_sums = lax.psum((grad_gain_attn, grad_gain_mlp), 'seq')]
    ppermute x51 -> x4, waiting for transfers between devices: 520 us -> 0.01 us  [shifted(): lax.ppermute(value, 'seq', [(source, source + steps) for source in range(...]
    dot_general x80 -> x12, matrix products: 212 us -> 42.1 us  [the longest x1 7.42 us: per_device(): up = jnp.dot(second, w_up, preferred_element_type=F32)]
    pallas_call x0 -> x1, Pallas kernels: none -> 136 us  [reduce_scatter(): pl.pallas_call(functools.partial(reduce_kernel, bits, lower, names), out_...]
    ppermute x51 -> x4, starting transfers between devices: 76.3 us -> 9.6 us  [shifted(): lax.ppermute(value, 'seq', [(source, source + steps) for source in range(...]
    dot_general x28 -> x7, matrix products: 40.1 us -> 13.9 us  [times_transpose(): lax.dot_general(left, weight, (((1,), (1,)), ((), ())), preferred_element...]
    concatenate x16 -> x1, local copies, waits for them, and re-layouts: 24.9 us -> 0.59 us  [per_device(): jnp.concatenate([grad_gain_attn[None], grad_gain_mlp[None], jnp.zeros((6,...]
    add x2 -> x0, local copies, waits for them, and re-layouts: 23.9 us -> none  [the longest x1 12 us: per_device(): grad_gate_w = grad_gate_w + outer_sum(second_rows, grad_gate)]
  transfers between devices with their start and end apart: 51 -> 4, of which waited for: 18 -> 0; matrix products, arithmetic and copies ran while one was open for 14% -> 11% of each run, Pallas kernels for 0% -> 0%
where the time goes in v1:
time: 335 us; the launch traced here: 331 us
  Pallas kernels  136 us (41%)
  local copies, waits for them, and re-layouts  111 us (33%)
  matrix products  58.4 us (17%)
  other arithmetic  14.3 us (4%)
  starting transfers between devices  9.6 us (3%)
    pallas_call x1, Pallas kernels, reduce_scatter(): pl.pallas_call(functools.partial(reduce_kernel, bits, lower, names), out_...  136 us
    unnamed x89, local copies, waits for them, and re-layouts  31.8 us
    dot_general x7, matrix products, times_transpose(): lax.dot_general(left, weight, (((1,), (1,)), ((), ())), preferred_element...  13.9 us
    slice x2, local copies, waits for them, and re-layouts, halves(): both[:, 1].reshape(rows_all, width)  11.8 us
    reshape x2, local copies, waits for them, and re-layouts, halves(): both = both.reshape(micro, 2, block, width)  11.4 us
    reshape x4, local copies, waits for them, and re-layouts, joined(): return both.reshape(micro, 2 * block, heads, HEAD)  11.1 us
    ppermute x4, starting transfers between devices, shifted(): lax.ppermute(value, 'seq', [(source, source + steps) for source in range(...  9.6 us
    dot_general x1, matrix products, per_device(): up = jnp.dot(second, w_up, preferred_element_type=F32)  7.42 us
  transfers between devices with their start and end apart: 4, of which 0 were waited for; matrix products, arithmetic and copies ran while one was open for 11% of the time, Pallas kernels for 0%

profile of v1, /device:TPU:0, one launch (start us, length us, event | category | flops | bytes accessed | tf_op | source)
XLA Modules:
  0.0 330.5 jit_solution(16294230351891950669)
XLA Ops:
  3.4 3.1 convolution_convert_fusion.5
  6.5 3.3 collective-permute-start
  10.5 3.8 %collective-permute-start.1 = (bf16[256,1024]{1,0:T(8,128)(2,1)S(1)}, bf16[256,1024]{1,0:T(8,128)(2,1)S(1)}, u32[]{:S(2)}, u32[]{:S(2)}) collective-permute-start(bf16[256,1024]{1,0:T(8,128)(2,1)S(1)} %convolution_convert_fusion.3), channel_id=1, source_target_pairs={{0,1},{1,2},{2,3},{3,4},{4,5},{5,6},{6,7},{7,8},{8,9},{9,10},{10,1... | collective-permute-start | bytes 1572872 | tf_op jit(solution)/shard_map/ppermute | solution.py:297
  23.0 2.3 reshape.194
  25.3 3.5 %copy.79 = bf16[4,128,16,64]{1,3,2,0:T(8,128)(2,1)} copy(bf16[4,128,16,64]{3,2,1,0:T(8,128)(2,1)} %reshape.194) | data formatting | bytes 2097152 | tf_op jit(solution)/shard_map/reshape | solution.py:334
  28.9 2.3 reshape.196
  31.2 2.9 copy.78
  34.2 2.4 fusion.29
  36.5 3.7 %fusion.8 = bf16[4,64,16,64]{1,3,2,0:T(8,128)(2,1)} fusion(bf16[4,128,16,64]{1,3,2,0:T(8,128)(2,1)} %copy.79, f32[4,16,64,128]{3,2,1,0:T(8,128)} %get-tuple-element.36, f32[4,16,64]{2,1,0:T(8,128)S(1)} %get-tuple-element.35), kind=kOutput, calls=%fused_computation.24 | convolution fusion | flops 68419584 | bytes 3686400 | tf_op jit(solution)/shard_map/bhqk,bkhd->bqhd/dot_general | solution.py:344
  42.9 2.6 multiply_reduce_fusion.5
  45.6 6.0 %fusion.30 = f32[256,2752]{0,1:T(8,128)} fusion(bf16[1024,2752]{0,1:T(8,128)(2,1)} %param.19, f32[256,1024]{1,0:T(8,128)S(1)} %get-tuple-element.38, f32[1024]{0:T(1024)S(1)} %copy-done.31, f32[256]{0:T(256)S(1)} %add_rsqrt_fusion.1), kind=kOutput, calls=%fused_computation.85 | convolution fusion | flops 1443627008 | bytes 9507840 | tf_op jit(solution)/shard_map/dot_general | solution.py:350
  51.5 3.4 %copy.82 = f32[256,2752]{1,0:T(8,128)} copy(f32[256,2752]{0,1:T(8,128)} %fusion.30) | data formatting | bytes 5636096 | tf_op jit(solution)/shard_map/dot_general | solution.py:350
  54.9 7.4 %fusion.2 = (bf16[2752,256]{1,0:T(8,128)(2,1)}, f32[256,2752]{0,1:T(8,128)}) fusion(f32[256,2752]{0,1:T(8,128)} %fusion.30, bf16[1024,2752]{0,1:T(8,128)(2,1)} %param.20, f32[256,1024]{1,0:T(8,128)S(1)} %get-tuple-element.38, f32[1024]{0:T(1024)S(1)} %copy-done.31, f32[256]{0:T(256)S(1)} %add_rsqrt_fusion.1), kind=kOutput, calls=%fused_computation.7 | convolution fusion | flops 1447854080 | bytes 13734912 | tf_op jit(solution)/shard_map/dot_general | solution.py:351
  62.3 3.5 %copy.83 = f32[256,2752]{1,0:T(8,128)} copy(f32[256,2752]{0,1:T(8,128)} %get-tuple-element.44) | data formatting | bytes 5636096 | tf_op jit(solution)/shard_map/dot_general | solution.py:351
  65.9 7.0 %fusion.11 = bf16[256,1024]{1,0:T(8,128)(2,1)} fusion(f32[256,1024]{1,0:T(8,128)S(1)} %get-tuple-element.38, bf16[2752,1024]{1,0:T(8,128)(2,1)} %param.21, f32[256,2752]{1,0:T(8,128)} %copy.83, f32[256,2752]{1,0:T(8,128)} %copy.82), kind=kOutput, calls=%fused_computation.31 | convolution fusion | flops 1447591936 | bytes 12845056 | tf_op jit(solution)/shard_map/dot_general | solution.py:355
  72.9 5.7 %multiply_convert_fusion = (bf16[256,2752]{1,0:T(8,128)(2,1)S(1)}, bf16[256,2752]{1,0:T(8,128)(2,1)S(1)}) fusion(f32[256,2752]{1,0:T(8,128)S(1)} %copy-done.15, f32[256,2752]{1,0:T(8,128)S(1)} %copy-done.16, bf16[256,1024]{1,0:T(8,128)(2,1)S(1)} %bitcast.158, bf16[2752,1024]{1,0:T(8,128)(2,1)} %param.21), kind=kOutput, calls=%fused_computation.1 | convolution fusion | flops 1451999232 | bytes 14614528 | tf_op jit(solution)/shard_map/dot_general | solution.py:285
  80.4 2.4 multiply_reduce_fusion.1
  87.2 2.7 copy.94
  89.9 4.0 %multiply_reduce_fusion = (f32[4,16,64]{2,1,0:T(8,128)S(1)}, f32[4,16,64,128]{3,2,1,0:T(8,128)S(1)}) fusion(f32[4,16,64,128]{3,2,1,0:T(8,128)} %get-tuple-element.36, f32[4,16,64]{2,1,0:T(8,128)S(1)} %get-tuple-element.35, bf16[4,64,16,64]{1,3,2,0:T(8,128)(2,1)} %copy.94, bf16[4,128,16,64]{1,3,2,0:T(8,128)(2,1)} %copy.79), kind=kOutput, calls=%fused_computation.14 | convolution fusion | flops 68677632 | bytes 5799936 | tf_op jit(solution)/shard_map/bqhd,bkhd->bhqk/dot_general | solution.py:366
  98.6 5.8 %reshape.215 = f32[4,2,64,1024]{2,1,3,0:T(2,128)} reshape(f32[4,128,16,64]{1,3,2,0:T(8,128)} %convolution_bitcast_fusion.1) | data formatting | bytes 4194304 | tf_op jit(solution)/shard_map/reshape | solution.py:375
  104.4 5.9 %slice.54 = f32[4,1,64,1024]{2,1,3,0:T(1,128)} slice(f32[4,2,64,1024]{2,1,3,0:T(2,128)} %reshape.215), slice={[0:4], [1:2], [0:64], [0:1024]} | slice | bytes 2097152 | tf_op jit(solution)/shard_map/slice | solution.py:376
  110.3 2.8 slice.55
  115.1 5.6 %reshape.216 = f32[4,2,64,1024]{2,1,3,0:T(2,128)} reshape(f32[4,128,16,64]{1,3,2,0:T(8,128)} %convolution_bitcast_fusion) | data formatting | bytes 4194304 | tf_op jit(solution)/shard_map/reshape | solution.py:375
  120.7 5.9 %slice.56 = f32[4,1,64,1024]{2,1,3,0:T(1,128)} slice(f32[4,2,64,1024]{2,1,3,0:T(2,128)} %reshape.216), slice={[0:4], [1:2], [0:64], [0:1024]} | slice | bytes 2097152 | tf_op jit(solution)/shard_map/slice | solution.py:376
  126.6 2.8 slice.57
  137.1 6.0 %copy.106 = f32[4,1,64,1024]{3,2,1,0:T(8,128)} copy(f32[4,1,64,1024]{2,1,3,0:T(1,128)} %slice.54) | data formatting | bytes 2097152
  143.0 5.6 %copy.107 = bf16[4,1,64,1024]{3,2,1,0:T(8,128)(2,1)} copy(bf16[4,1,64,1024]{2,1,3,0:T(2,128)(2,1)} %slice.55) | data formatting | bytes 1048576
  150.0 5.8 %copy.108 = f32[4,1,64,1024]{3,2,1,0:T(8,128)} copy(f32[4,1,64,1024]{2,1,3,0:T(1,128)} %slice.56) | data formatting | bytes 2097152
  155.8 5.6 %copy.109 = bf16[4,1,64,1024]{3,2,1,0:T(8,128)(2,1)} copy(bf16[4,1,64,1024]{2,1,3,0:T(2,128)(2,1)} %slice.57) | data formatting | bytes 1048576
  162.7 2.3 reshape.203
  179.9 135.8 %weight_grads.1 = (f32[96,1024]{1,0:T(8,128)}, f32[32,2816]{1,0:T(8,128)}, f32[32,2816]{1,0:T(8,128)}, f32[32,1024]{1,0:T(8,128)}, f32[32,2048]{1,0:T(8,128)}, /*index=5*/f32[32,1024]{1,0:T(8,128)}, f32[8,1024]{1,0:T(8,128)}) custom-call(bf16[2,16,96,256]{3,2,1,0:T(8,128)(2,1)} %pad.11.refs_0_, bf16[2,16,32,256]{3,2,1,0:T(8,128)(2,1)} %bitcast.159, ...), custom_call_target="tpu_custom_call" | custom-call | tf_op jit(solution)/shard_map/weight_grads/pallas_call | solution.py:269
  327.4 2.7 multiply_add_fusion
  (150 shorter events, 64.5 us)
Async XLA Ops:
  2.0 7.8 %copy-start.19 = (bf16[1024,1024]{1,0:T(8,128)(2,1)S(1)}, bf16[1024,1024]{1,0:T(8,128)(2,1)}, u32[]{:S(2)}) copy-start(bf16[1024,1024]{1,0:T(8,128)(2,1)} %param.16) | copy-start | bytes 6291460
  6.5 7.9 %copy-start.34 = (s32[4,8]{1,0:T(4,128)S(1)}, s32[4,8]{1,0:T(4,128)}, u32[]{:S(2)}) copy-start(s32[4,8]{1,0:T(4,128)} %param.23) | copy-start | bytes 388
  6.5 15.2 %collective-permute-start = (bf16[256,1024]{1,0:T(8,128)(2,1)}, bf16[256,1024]{1,0:T(8,128)(2,1)}, u32[]{:S(2)}, u32[]{:S(2)}) collective-permute-start(bf16[256,1024]{1,0:T(8,128)(2,1)} %convolution_convert_fusion.5), channel_id=1, source_target_pairs={{0,1},{1,2},{2,3},{3,4},{4,5},{5,6},{6,7},{7,8},{8,9},{9,10},{10,1... | collective-permute-start | bytes 1572872 | tf_op jit(solution)/shard_map/ppermute | solution.py:297
  10.5 18.3 %collective-permute-start.1 = (bf16[256,1024]{1,0:T(8,128)(2,1)S(1)}, bf16[256,1024]{1,0:T(8,128)(2,1)S(1)}, u32[]{:S(2)}, u32[]{:S(2)}) collective-permute-start(bf16[256,1024]{1,0:T(8,128)(2,1)S(1)} %convolution_convert_fusion.3), channel_id=1, source_target_pairs={{0,1},{1,2},{2,3},{3,4},{4,5},{5,6},{6,7},{7,8},{8,9},{9,10},{10,1... | collective-permute-start | bytes 1572872 | tf_op jit(solution)/shard_map/ppermute | solution.py:297
  31.2 2.9 copy-start.13
  40.2 2.7 copy-start.2
  42.9 2.6 copy-start.4
  42.9 2.6 copy-start.31
  65.8 7.0 %copy-start.6 = (bf16[4,64,1024]{2,1,0:T(8,128)(2,1)S(1)}, bf16[4,64,1024]{2,1,0:T(8,128)(2,1)}, u32[]{:S(2)}) copy-start(bf16[4,64,1024]{2,1,0:T(8,128)(2,1)} %param.22) | copy-start | bytes 1572868
  65.8 7.0 %copy-start.15 = (f32[256,2752]{1,0:T(8,128)S(1)}, f32[256,2752]{1,0:T(8,128)}, u32[]{:S(2)}) copy-start(f32[256,2752]{1,0:T(8,128)} %copy.82) | copy-start | bytes 8454148
  65.8 7.0 %copy-start.16 = (f32[256,2752]{1,0:T(8,128)S(1)}, f32[256,2752]{1,0:T(8,128)}, u32[]{:S(2)}) copy-start(f32[256,2752]{1,0:T(8,128)} %copy.83) | copy-start | bytes 8454148
  65.9 12.8 %slice-start = ((s8[5636096]{0:T(1024)(128)(4,1)}), s8[4194304]{0:T(1024)(128)(4,1)S(1)}, s32[]{:S(2)}) async-start(s8[5636096]{0:T(1024)(128)(4,1)} %bitcast.153), calls=%async_computation | async-start | bytes 8388608
  65.9 14.5 %slice-start.2 = ((s8[5636096]{0:T(1024)(128)(4,1)}), s8[4194304]{0:T(1024)(128)(4,1)S(1)}, s32[]{:S(2)}) async-start(s8[5636096]{0:T(1024)(128)(4,1)} %bitcast.179), calls=%async_computation.2 | async-start | bytes 8388608
  72.9 5.8 %slice-start.1 = ((s8[5636096]{0:T(1024)(128)(4,1)}), s8[1441792]{0:T(1024)(128)(4,1)S(1)}, s32[]{:S(2)}) async-start(s8[5636096]{0:T(1024)(128)(4,1)} %bitcast.153), calls=%async_computation.1 | async-start | bytes 2883584
  72.9 7.5 %slice-start.3 = ((s8[5636096]{0:T(1024)(128)(4,1)}), s8[1441792]{0:T(1024)(128)(4,1)S(1)}, s32[]{:S(2)}) async-start(s8[5636096]{0:T(1024)(128)(4,1)} %bitcast.179), calls=%async_computation.3 | async-start | bytes 2883584
  89.9 4.0 %copy-start.23 = (f32[4,16,64,128]{3,2,1,0:T(8,128)S(1)}, f32[4,16,64,128]{3,2,1,0:T(8,128)}, u32[]{:S(2)}) copy-start(f32[4,16,64,128]{3,2,1,0:T(8,128)} %get-tuple-element.36) | copy-start | bytes 6291460
  104.4 5.9 %copy-start = (f32[4,2,64,1024]{2,1,3,0:T(2,128)S(1)}, f32[4,2,64,1024]{2,1,3,0:T(2,128)}, u32[]{:S(2)}) copy-start(f32[4,2,64,1024]{2,1,3,0:T(2,128)} %reshape.215) | copy-start | bytes 6291460
  110.2 2.8 copy-start.24
  110.2 2.8 copy-start.29
  120.7 5.9 %copy-start.1 = (f32[4,2,64,1024]{2,1,3,0:T(2,128)S(1)}, f32[4,2,64,1024]{2,1,3,0:T(2,128)}, u32[]{:S(2)}) copy-start(f32[4,2,64,1024]{2,1,3,0:T(2,128)} %reshape.216) | copy-start | bytes 6291460
  126.6 3.7 %copy-start.28 = (bf16[256,2752]{1,0:T(8,128)(2,1)S(1)}, bf16[256,2752]{1,0:T(8,128)(2,1)}, u32[]{:S(2)}) copy-start(bf16[256,2752]{1,0:T(8,128)(2,1)} %copy-done.27) | copy-start | bytes 4227076
  137.1 34.0 %copy-start.3 = (bf16[256,1024]{1,0:T(8,128)(2,1)}, bf16[256,1024]{1,0:T(8,128)(2,1)S(1)}, u32[]{:S(2)}) copy-start(bf16[256,1024]{1,0:T(8,128)(2,1)S(1)} %convert_element_type.121.refs_7_) | copy-start | bytes 1572868
  148.7 23.1 %collective-permute-start.2 = (bf16[256,1024]{1,0:T(8,128)(2,1)}, bf16[256,1024]{1,0:T(8,128)(2,1)}, u32[]{:S(2)}, u32[]{:S(2)}) collective-permute-start(bf16[256,1024]{1,0:T(8,128)(2,1)} %bitcast.15), channel_id=1, source_target_pairs={{1,0},{2,1},{3,2},{4,3},{5,4},{6,5},{7,6},{8,7},{9,8},{10,9},{11,1... | collective-permute-start | bytes 1572872 | tf_op jit(solution)/shard_map/ppermute | solution.py:297
  161.4 13.0 %collective-permute-start.3 = (bf16[256,1024]{1,0:T(8,128)(2,1)}, bf16[256,1024]{1,0:T(8,128)(2,1)}, u32[]{:S(2)}, u32[]{:S(2)}) collective-permute-start(bf16[256,1024]{1,0:T(8,128)(2,1)} %bitcast.18), channel_id=1, source_target_pairs={{1,0},{2,1},{3,2},{4,3},{5,4},{6,5},{7,6},{8,7},{9,8},{10,9},{11,1... | collective-permute-start | bytes 1572872 | tf_op jit(solution)/shard_map/ppermute | solution.py:297
  165.1 3.5 %copy-start.5 = (bf16[256,1024]{1,0:T(8,128)(2,1)S(1)}, bf16[256,1024]{1,0:T(8,128)(2,1)}, u32[]{:S(2)}) copy-start(bf16[256,1024]{1,0:T(8,128)(2,1)} %copy-done.4) | copy-start | bytes 1572868
  168.8 2.3 copy-start.18
  171.0 2.5 copy-start.20
  174.3 3.0 copy-start.21
  174.4 3.0 copy-start.32
  315.7 9.0 %copy-start.30 = (f32[32,2816]{1,0:T(8,128)S(1)}, f32[32,2816]{1,0:T(8,128)}, u32[]{:S(2)}) copy-start(f32[32,2816]{1,0:T(8,128)} %get-tuple-element.23) | copy-start | bytes 1081348
  318.7 8.6 %copy-start.7 = (bf16[4,64,1024]{2,1,0:T(8,128)(2,1)S(1)}, bf16[4,64,1024]{2,1,0:T(8,128)(2,1)}, u32[]{:S(2)}) copy-start(bf16[4,64,1024]{2,1,0:T(8,128)(2,1)} %param.22) | copy-start | bytes 1572868
  318.7 8.6 %copy-start.11 = (f32[256,1024]{1,0:T(8,128)S(1)}, f32[256,1024]{1,0:T(8,128)}, u32[]{:S(2)}) copy-start(f32[256,1024]{1,0:T(8,128)} %get-tuple-element.42) | copy-start | bytes 3145732
  (12 other events, 19.1 us)

commit v2 on v1

v2 whole, which is shorter than its diff:
```python
import functools
import math

import jax
import jax.numpy as jnp
from jax import lax
from jax.experimental import pallas as pl
from jax.experimental.pallas import tpu as pltpu
from jax.sharding import PartitionSpec as P

HEAD = 64
WIN = 64
EPSILON = 1e-05
MESH = pl.DeviceIdType.MESH
MOST_GROUPS = 32
CHUNK = 256
BF16 = jnp.bfloat16
F32 = jnp.float32

MATRICES = {
    "down": (("hidden", "cot"),),
    "gate": (("second", "dgate"),),
    "up": (("second", "dup"),),
    "query": (("first", "dquery"),),
    "keyval": (("first", "dkeyval"), ("before", "dkvback")),
    "out": (("attended", "branch"),),
}
ROWS = ("first", "before", "attended", "second", "hidden")
COLS = ("cot", "dgate", "dup", "branch", "dquery", "dkeyval", "dkvback")
NAMES = tuple(MATRICES)
INDEX = {name: index for index, name in enumerate(NAMES)}


def round_up(value, unit):
    return -(-value // unit) * unit


def bit_orders(bits):
    ascending = list(range(1, bits + 1))
    swapped = [2, 1] + ascending[2:]
    last_first = ascending[2:] + [1, 2]
    return {
        "down": last_first,
        "gate": ascending,
        "query": ascending,
        "out": ascending,
        "up": swapped,
        "keyval": swapped,
    }


def bit_of(number, bit):
    return (number // (1 << bit)) % 2


def flip(number, bit):
    return number + (1 << bit) * (1 - 2 * bit_of(number, bit))


def dot(left, right):
    return jnp.dot(left, right, preferred_element_type=F32)


def dot_rows(left, right):
    return lax.dot_general(left, right, (((1,), (1,)), ((), ())), preferred_element_type=F32)


def dot_cols(left, right):
    return lax.dot_general(left, right, (((0,), (0,)), ((), ())), preferred_element_type=F32)


def at_chunk(index, size=CHUNK):
    return pl.ds(index * size, size)


def loop(first, last, body, **options):
    def step(at, carry):
        body(at)
        return carry

    lax.fori_loop(first, last, step, 0, **options)


def layer_kernel(sizes, in_names, out_names, scratch_names, *refs):
    micro, block, width, hidden_width, devices, groups = sizes
    r = dict(zip(in_names + out_names + scratch_names, refs))
    lower = devices // groups
    bits = groups.bit_length() - 2
    count = 1 << bits
    half = count // 2
    orders = bit_orders(bits)
    rows_all = micro * block
    chunks = width // CHUNK
    full = hidden_width // CHUNK
    tail = hidden_width % CHUNK
    depth = r["ring_gate"].shape[0]
    kept = full - depth
    scale = 1.0 / math.sqrt(HEAD)

    position = lax.axis_index("seq")
    me, rest = position // lower, position % lower
    core = me % 2
    my_unit = me // 2
    after = ((position + 1) % devices,)
    behind = ((position + devices - 1) % devices,)

    def partner(bit):
        return (flip(me, bit) * lower + rest,)


    def local_copy(source, target, index):
        return pltpu.make_async_copy(source, target, r["local_sem"].at[index])

    def remote_copy(source, target, sems, index, device):
        send, recv = r[sems + "_send"], r[sems + "_recv"]
        return pltpu.make_async_remote_copy(
            src_ref=source, dst_ref=target, send_sem=send.at[index], recv_sem=recv.at[index],
            device_id=device, device_id_type=MESH,
        )

    load_tokens = local_copy(r["tokens"], r["x"], 0)
    load_cot = local_copy(r["cotangent"], r["col_cot"].at[0], 1)
    load_out = local_copy(r["w_out"], r["wo"], 2)
    rings = ("ring_gate", "ring_up", "ring_down")
    past = pl.ds(full * CHUNK, tail)
    load_tails = [
        local_copy(r[name].at[past, :], r["tail_" + name[2:]], 3 + index)
        for index, name in enumerate(("w_gate", "w_up", "w_down"))
    ]
    def attention_weights(base):
        return [
            pltpu.make_async_copy(
                r[name].at[at_chunk(slot), :], r[ring].at[slot], r["ring_sem"].at[index, base + slot]
            )
            for index, (name, ring) in enumerate(zip(("w_query", "w_key", "w_value"), rings))
            for slot in range(depth)
        ]

    attention_first = attention_weights(2 * full)
    attention_again = attention_weights(2 * full + depth)

    def hidden_weights(chunk, place):
        slot = place % depth
        return [
            pltpu.make_async_copy(r[name].at[at_chunk(chunk), :], r[ring].at[slot], r["ring_sem"].at[index, place])
            for index, (name, ring) in enumerate(zip(("w_gate", "w_up", "w_down"), rings))
        ]

    padded = r["col_dgate"].shape[2]

    def pair_copies():
        plan = {}
        for name in ROWS:
            plan[name] = (r["row_" + name].at[:, 1 - core], r["peer_" + name])
        plan["cot"] = (r["cotangent"], r["col_cot"].at[1])
        for name in ("dgate", "dup", "branch", "dquery", "dkeyval", "dkvback"):
            plan[name] = (r["col_" + name].at[0], r["col_" + name].at[1])
        return {
            name: remote_copy(source, target, "pair", index, partner(0))
            for index, (name, (source, target)) in enumerate(plan.items())
        }

    pair = pair_copies()
    ready = set()

    def need(name):
        if name not in ready:
            ready.add(name)
            pair[name].wait_recv()

    halo_out = remote_copy(r["tokens"], r["x_before"], "halo", 0, after)
    halo_back = remote_copy(r["back_out"], r["back_in"], "halo", 1, behind)

    load_tokens.start()
    for copy in attention_first:
        copy.start()
    load_out.start()
    load_cot.start()
    for copy in load_tails:
        copy.start()
    barrier = pltpu.get_barrier_semaphore()
    for device in [after, behind] + [partner(bit) for bit in range(bits + 1)]:
        pl.semaphore_signal(barrier, inc=1, device_id=device, device_id_type=MESH)
    pl.semaphore_wait(barrier, bits + 3)
    halo_out.start()
    pair["cot"].start()
    for name in ("dgate", "dup"):
        r["col_" + name][0, :, pl.ds(full * CHUNK, padded - full * CHUNK)] = jnp.zeros(
            (rows_all, padded - full * CHUNK), BF16
        )


    def unit_at(order, slot):
        unit = my_unit
        for place, bit in enumerate(order):
            rel = (slot // (1 << (bits - 1 - place))) % 2
            unit = unit + (1 << (bit - 1)) * rel * (1 - 2 * bit_of(me, bit))
        return unit

    def product(name, first, last, store):
        units = [unit_at(orders[name], slot) for slot in range(first, last)]
        pairs = []
        for row, col in MATRICES[name]:
            need(row)
            need(col)
            for source in range(2):
                parts = [
                    r["row_" + row][unit, core] if source == 0 else r["peer_" + row][unit] for unit in units
                ]
                pairs.append((jnp.concatenate(parts, axis=0), r["col_" + col], source))
        unit_rows = r["row_" + MATRICES[name][0][0]].shape[2]

        def body(at):
            lanes = at_chunk(at)
            total = None
            for left, ref, source in pairs:
                term = dot(left, ref[source, :, lanes])
                total = term if total is None else total + term
            store(lanes, total.reshape(last - first, unit_rows, CHUNK))

        loop(0, pairs[0][1].shape[2] // CHUNK, body)

    def step_copy(name, level, slot):
        size = half >> level
        source = r["send_" + name].at[slot] if level == 0 else r[f"land_{name}{level - 1}"].at[size + slot]
        return remote_copy(
            source, r[f"land_{name}{level}"].at[slot], "step", (INDEX[name], count - 2 * size + slot),
            partner(orders[name][level]),
        )

    def send_product(name):
        target = r["send_" + name]

        def store(lanes, value):
            target[:, :, lanes] = value.astype(BF16)

        product(name, half, count, store)
        loop(0, half, lambda at: step_copy(name, 0, (at + half // 2) % half).start())

    def finish(name, total):
        flat = r["flat_" + name]
        if name in ("gate", "up"):
            rows, wide = total.shape
            turn = r["turn"]
            for j in range(wide // 128):
                turn[pl.ds(rows * j, rows), :] = total[:, 128 * j : 128 * (j + 1)]
            few = rows // 2
            steps = hidden_width // 64
            whole = hidden_width // 128
            even = [turn[pl.ds(rows * j, few, stride=2), :] for j in range(whole + 1)]
            odd = [pltpu.roll(turn[pl.ds(rows * j + 1, few, stride=2), :], 64, 1) for j in range(whole + 1)]
            low = lax.broadcasted_iota(jnp.int32, (few, 128), 1) < 64
            for j in range(whole):
                flat[pl.ds(j, few, stride=steps), :] = even[j]
                flat[pl.ds(whole + 1 + j, few, stride=steps), :] = jnp.where(low, odd[j], odd[j + 1])
            flat[pl.ds(whole, few, stride=steps), :] = jnp.where(low, even[whole], odd[0])
            return
        parts = ((flat, 0),)
        if name == "keyval":
            parts = ((flat, 0), (r["flat_value"], width))
        per_row = width // 128
        for ref, base in parts:
            rows = ref.shape[0] // per_row
            for j in range(per_row):
                ref[pl.ds(j, rows, stride=per_row), :] = total[:rows, base + 128 * j : base + 128 * (j + 1)]

    def arrive(name, level, first, last, forward):
        size = half >> level
        buffer = r[f"land_{name}{level}"]
        if level == 0:
            loop(first, last, lambda slot: step_copy(name, 0, slot).wait_recv())

            def store(lanes, value):
                buffer[first:last, :, lanes] = (value + buffer[first:last, :, lanes].astype(F32)).astype(BF16)

            product(name, first, last, store)
            if forward:
                loop(first, last, lambda slot: step_copy(name, 1, slot - size // 2).start())
            return
        before = r[f"land_{name}{level - 1}"]

        def body(slot):
            step_copy(name, level, slot).wait_recv()
            total = buffer[slot].astype(F32) + before[slot].astype(F32)
            if level == bits - 1:
                finish(name, total)
            else:
                buffer[slot] = total.astype(BF16)
            if forward:
                step_copy(name, level + 1, slot - size // 2).start()

        loop(first, last, body)

    def gain_copy(bit):
        return remote_copy(r["gain_buf"].at[2 * bit], r["gain_buf"].at[2 * bit + 1], "gain", bit, partner(bit))

    def gain_step(bit):
        gain_copy(bit).wait_recv()
        total = r["gain_buf"][2 * bit] + r["gain_buf"][2 * bit + 1]
        if bit < bits:
            r["gain_buf"][2 * bit + 2] = total
            gain_copy(bit + 1).start()
        else:
            for row, name in enumerate(("gain_attn_sum", "gain_mlp_sum")):
                for j in range(width // 128):
                    r[name][j : j + 1, :] = total[row : row + 1, 128 * j : 128 * (j + 1)]


    def some_rows(at):
        return pl.ds(at * block, block)

    def row_scale(value):
        return lax.rsqrt(jnp.mean(value * value, axis=-1, keepdims=True) + EPSILON)

    def first_norm(source, target):
        def body(at):
            value = source[some_rows(at), :].astype(F32)
            target[some_rows(at), :] = (value * row_scale(value) * r["gain_attn"][...]).astype(BF16)

        loop(0, micro, body)

    def by_owner(name, source):
        ref = r["row_" + name]
        ref[...] = source[...].T.reshape(ref.shape)
        pair[name].start()

    def project(left, ring, target):
        def body(at):
            total = dot(left[:, at_chunk(0)], r[ring][0, :, at_chunk(at)])
            for part in range(1, chunks):
                total += dot(left[:, at_chunk(part)], r[ring][part, :, at_chunk(at)])
            target[:, at_chunk(at)] = total.astype(BF16)

        loop(0, chunks, body)

    act, other = r["act"], r["other"]
    load_tokens.wait()
    first_norm(r["x"], act)
    by_owner("first", act)
    for index, (ring, target) in enumerate(zip(rings, ("queries", "keys", "values"))):
        for copy in attention_first[index * depth : (index + 1) * depth]:
            copy.wait()
        project(act, ring, r[target])
    halo_out.wait_recv()
    first_norm(r["x_before"], other)
    by_owner("before", other)
    project(other, "ring_up", r["keys_before"])
    project(other, "ring_down", r["values_before"])
    for slot in range(depth):
        for copy in hidden_weights(slot, slot):
            copy.start()

    quad = CHUNK // HEAD
    start = position * block
    lane_head = lax.broadcasted_iota(jnp.int32, (block, CHUNK), 1) // HEAD
    key_at = start - WIN + lax.broadcasted_iota(jnp.int32, (2 * block, CHUNK), 0)
    query_at = start + lax.broadcasted_iota(jnp.int32, (1, CHUNK), 1) % block

    def stacked(value):
        return jnp.concatenate([jnp.where(lane_head == h, value, jnp.zeros_like(value)) for h in range(quad)], axis=0)

    def unstacked(value):
        total = jnp.zeros((block, CHUNK), F32)
        for h in range(quad):
            total = jnp.where(lane_head == h, value[h * block : (h + 1) * block], total)
        return total

    def unit(index):
        return index // chunks, some_rows(index // chunks), at_chunk(index % chunks)

    def both(before, own, rows, lanes):
        return jnp.concatenate([r[before][rows, lanes], r[own][rows, lanes]], axis=0)

    def allowed(which):
        def body(at, carry):
            end, low = carry
            end = end + r["lengths"][which, at]
            return end, jnp.where(query_at >= end, end, low)

        _, low = lax.fori_loop(
            0, r["lengths"].shape[1], body, (jnp.int32(0), jnp.zeros((1, CHUNK), jnp.int32))
        )
        low = jnp.maximum(low, query_at - (WIN - 1))
        return (key_at >= low) & (key_at <= query_at)

    def scores(which, keys, queries):
        return jnp.where(allowed(which), dot_rows(keys, queries) * scale, -1e30)

    def attend(index):
        which, rows, lanes = unit(index)
        logits = scores(which, both("keys_before", "keys", rows, lanes), stacked(r["queries"][rows, lanes]))
        peak = jnp.max(logits, axis=0, keepdims=True)
        powers = jnp.exp(logits - peak)
        total = jnp.sum(powers, axis=0, keepdims=True)
        r["log_sums"][index] = jnp.broadcast_to(peak + jnp.log(total), (8, CHUNK))
        probability = (powers / total).astype(BF16)
        mixed = dot_cols(probability, both("values_before", "values", rows, lanes))
        act[rows, lanes] = unstacked(mixed).astype(BF16)

    loop(0, micro * chunks, attend)
    by_owner("attended", act)
    load_out.wait()
    middle = r["input_grad"]

    def out_project(at):
        lanes = at_chunk(at)
        middle[:, lanes] = r["x"][:, lanes].astype(F32) + dot(act[...], r["wo"][:, lanes])

    loop(0, chunks, out_project)

    def second_norm(at):
        value = middle[some_rows(at), :]
        other[some_rows(at), :] = (value * row_scale(value) * r["gain_mlp"][...]).astype(BF16)

    loop(0, micro, second_norm)
    by_owner("second", other)


    def hidden_part(gate, up, grad_hidden):
        sigmoid = jax.nn.sigmoid(gate)
        silu = gate * sigmoid
        hidden = (silu * up).astype(BF16)
        dgate = (grad_hidden * up * sigmoid * (1.0 + gate * (1.0 - sigmoid))).astype(BF16)
        return hidden, dgate, (grad_hidden * silu).astype(BF16)

    columns = r["columns"]

    def hidden_chunk(at, prefetch):
        slot = at % depth
        for copy in hidden_weights(at, at):
            copy.wait()
        hidden, dgate, dup = hidden_part(
            dot_rows(other[...], r["ring_gate"][slot]),
            dot_rows(other[...], r["ring_up"][slot]),
            dot_rows(r["col_cot"][0], r["ring_down"][slot]),
        )
        lanes = at_chunk(at)
        r["hidden"][:, lanes] = hidden
        r["col_dgate"][0, :, lanes] = dgate
        r["col_dup"][0, :, lanes] = dup
        columns[lanes, :] = hidden.astype(F32).T
        if prefetch:
            for copy in hidden_weights(at + depth, at + depth):
                copy.start()

    load_cot.wait()
    for copy in load_tails:
        copy.wait()
    for at in range(full):
        hidden_chunk(at, at < kept)
    hidden, dgate, dup = hidden_part(
        dot_rows(other[...], r["tail_gate"][...]),
        dot_rows(other[...], r["tail_up"][...]),
        dot_rows(r["col_cot"][0], r["tail_down"][...]),
    )
    r["hidden"][:, past] = hidden
    r["col_dgate"][0, :, past] = dgate
    r["col_dup"][0, :, past] = dup
    r["square"][...] = jnp.zeros_like(r["square"])
    r["square"][:, :tail] = hidden.astype(F32)
    columns[pl.ds(full * CHUNK, CHUNK), :] = r["square"][...].T
    own_rows = hidden_width // groups
    held_rows = r["row_hidden"].shape[2]
    for owner in range(groups):
        r["row_hidden"][owner // 2, owner % 2] = columns[pl.ds(owner * own_rows, held_rows), :].astype(BF16)
    pair["hidden"].start()
    pair["dgate"].start()
    pair["dup"].start()
    send_product("down")
    send_product("gate")
    send_product("up")


    sums = [pl.ds(n * CHUNK, CHUNK) for n in range(2 * chunks)]

    def fold(hidden, dgate, dup, gate_ref, up_ref, down_ref):
        back = dot(dgate, gate_ref[...]) + dot(dup, up_ref[...])
        onward = dot(hidden, down_ref[...])
        for n in range(chunks):
            columns[sums[n], :] += back[:, n * CHUNK : (n + 1) * CHUNK]
            columns[sums[chunks + n], :] += onward[:, n * CHUNK : (n + 1) * CHUNK]

    def fold_chunk(at, arrived, prefetch):
        slot = at % depth
        chunk = at - depth if arrived else at - depth - full
        if not arrived:
            for copy in hidden_weights(chunk, at):
                copy.wait()
        lanes = at_chunk(chunk)
        fold(
            r["hidden"][:, lanes], r["col_dgate"][0, :, lanes], r["col_dup"][0, :, lanes],
            *(r[ring].at[slot] for ring in rings),
        )
        if prefetch:
            for copy in hidden_weights(at - full, at + depth):
                copy.start()

    for some in sums:
        columns[some, :] = jnp.zeros((CHUNK, CHUNK), F32)
    fold(
        r["hidden"][:, past], r["col_dgate"][0, :, past], r["col_dup"][0, :, past],
        r["tail_gate"], r["tail_up"], r["tail_down"],
    )
    for at in range(full, 2 * full):
        fold_chunk(at, at < full + depth, at < full + kept)
    for copy in attention_again:
        copy.start()

    def summed(at, base):
        return jnp.concatenate(
            [columns[pl.ds((base + n) * CHUNK + at * block, block), :] for n in range(chunks)],
            axis=1,
        )

    def norm_backward(grad, value, gain):
        inverse = row_scale(value)
        normed = value * inverse
        scaled = grad * gain
        mean = jnp.mean(scaled * normed, axis=-1, keepdims=True)
        return inverse * (scaled - normed * mean), jnp.sum(grad * normed, axis=0, keepdims=True)

    def middle_backward(at, gain_sum):
        rows = some_rows(at)
        value = middle[rows, :]
        r["output"][rows, :] = (value + summed(at, chunks)).astype(BF16)
        grad, part = norm_backward(summed(at, 0), value, r["gain_mlp"][...])
        grad = grad + r["col_cot"][0, rows, :].astype(F32)
        middle[rows, :] = grad
        r["col_branch"][0, rows, :] = grad.astype(BF16)
        return gain_sum + part

    gain_mlp_sum = lax.fori_loop(0, micro, middle_backward, jnp.zeros((1, width), F32))
    pair["branch"].start()

    def attended_backward(at):
        r["grad_attended"][:, at_chunk(at)] = dot_rows(r["col_branch"][0], r["wo"][at_chunk(at), :]).astype(BF16)

    loop(0, chunks, attended_backward)


    def attend_backward(index):
        which, rows, lanes = unit(index)
        keys = both("keys_before", "keys", rows, lanes)
        values = both("values_before", "values", rows, lanes)
        queries = stacked(r["queries"][rows, lanes])
        grads = stacked(r["grad_attended"][rows, lanes])
        probability = jnp.exp(scores(which, keys, queries) - r["log_sums"][index][:1])
        grad_prob = dot_rows(values, grads)
        delta = jnp.sum(probability * grad_prob, axis=0, keepdims=True)
        grad_scores = (scale * probability * (grad_prob - delta)).astype(BF16)
        r["col_dquery"][0, rows, lanes] = unstacked(dot_cols(grad_scores, keys)).astype(BF16)
        dkey = dot(grad_scores, queries).astype(BF16)
        dvalue = dot(probability.astype(BF16), grads).astype(BF16)
        lanes_value = at_chunk(chunks + index % chunks)
        r["col_dkvback"][0, rows, lanes] = dkey[:block]
        r["col_dkvback"][0, rows, lanes_value] = dvalue[:block]
        r["col_dkeyval"][0, rows, lanes] = dkey[block:]
        r["col_dkeyval"][0, rows, lanes_value] = dvalue[block:]

    loop(0, micro * chunks, attend_backward)
    for name in ("dquery", "dkeyval", "dkvback"):
        pair[name].start()
    send_product("out")

    def through_keys(ref, at):
        return dot_rows(ref[0, :, :width], r["ring_up"][at]) + dot_rows(ref[0, :, width:], r["ring_down"][at])

    def back_chunk(at):
        r["back_out"][:, at_chunk(at)] = through_keys(r["col_dkvback"], at).astype(BF16)

    def first_chunk(at):
        columns[at_chunk(at), :] = through_keys(r["col_dkeyval"], at) + dot_rows(
            r["col_dquery"][0], r["ring_gate"][at]
        )

    for copy in attention_again:
        copy.wait()
    loop(0, chunks, back_chunk)
    pl.when(position > 0)(halo_back.start)
    send_product("query")
    send_product("keyval")
    loop(0, chunks, first_chunk)


    def input_backward(at, gain_sum):
        rows = some_rows(at)
        back = jnp.where(position < devices - 1, r["back_in"][rows, :].astype(F32), 0.0)
        grad = summed(at, 0) + back
        grad, part = norm_backward(grad, r["x"][rows, :].astype(F32), r["gain_attn"][...])
        middle[rows, :] = middle[rows, :] + grad
        return gain_sum + part

    turn = ("gate", "up", "down", "query", "keyval", "out")
    for level in range(bits):
        size = half >> level
        if level > 0:
            gain_step(level - 1)
        for name in turn:
            if size > 1:
                arrive(name, level, size // 2, size, True)
        for name in turn:
            arrive(name, level, 0, max(size // 2, 1), False)
        if level == 0:
            pl.when(position < devices - 1)(halo_back.wait_recv)
            gain_attn_sum = lax.fori_loop(0, micro, input_backward, jnp.zeros((1, width), F32))
            r["gain_buf"][0] = jnp.concatenate(
                [gain_attn_sum, gain_mlp_sum, jnp.zeros((6, width), F32)], axis=0
            )
            gain_copy(0).start()
    gain_step(bits - 1)
    gain_step(bits)

    halo_out.wait_send()
    pl.when(position > 0)(halo_back.wait_send)
    for copy in pair.values():
        copy.wait_send()
    for bit in range(bits + 1):
        gain_copy(bit).wait_send()
    for name in NAMES:
        for level in range(bits):
            loop(0, half >> level, lambda slot: step_copy(name, level, slot).wait_send())


def layer(tokens, gain_attn, gain_mlp, weights, cotangent, lengths, micro, devices, groups):
    rows_all, width = tokens.shape
    hidden_width = weights["w_gate"].shape[0]
    block = rows_all // micro
    bits = groups.bit_length() - 2
    count = 1 << bits
    half = count // 2
    chunks = width // CHUNK
    padded = round_up(hidden_width, CHUNK)
    tail = hidden_width % CHUNK
    depth = chunks
    unit_rows = {name: width // groups for name in ROWS}
    unit_rows["hidden"] = round_up(hidden_width // groups, 16)
    widths = {name: width for name in COLS}
    widths.update(dgate=padded, dup=padded, dkeyval=2 * width, dkvback=2 * width)

    inputs = {"tokens": tokens, "cotangent": cotangent, **weights}
    any_spec = pl.BlockSpec(memory_space=pl.ANY)
    vmem_spec = pl.BlockSpec(memory_space=pltpu.VMEM)
    in_specs = [any_spec] * len(inputs) + [vmem_spec] * 2 + [pl.BlockSpec(memory_space=pltpu.SMEM)]
    inputs.update(gain_attn=gain_attn[None], gain_mlp=gain_mlp[None], lengths=lengths)

    outs = {
        "output": ((rows_all, width), BF16),
        "input_grad": ((rows_all, width), F32),
        "gain_attn_sum": ((width // 128, 128), F32),
        "gain_mlp_sum": ((width // 128, 128), F32),
    }
    own = {"query": width * width, "keyval": width * width, "value": width * width, "out": width * width}
    own.update(gate=width * hidden_width, up=width * hidden_width, down=width * hidden_width)
    for name, size in own.items():
        outs["flat_" + name] = ((size // groups // 128, 128), F32)

    scratch = {
        "x": pltpu.VMEM((rows_all, width), BF16),
        "x_before": pltpu.VMEM((rows_all, width), BF16),
        "act": pltpu.VMEM((rows_all, width), BF16),
        "other": pltpu.VMEM((rows_all, width), BF16),
        "queries": pltpu.VMEM((rows_all, width), BF16),
        "keys": pltpu.VMEM((rows_all, width), BF16),
        "values": pltpu.VMEM((rows_all, width), BF16),
        "keys_before": pltpu.VMEM((rows_all, width), BF16),
        "values_before": pltpu.VMEM((rows_all, width), BF16),
        "grad_attended": pltpu.VMEM((rows_all, width), BF16),
        "back_out": pltpu.VMEM((rows_all, width), BF16),
        "back_in": pltpu.VMEM((rows_all, width), BF16),
        "log_sums": pltpu.VMEM((micro * chunks, 8, CHUNK), F32),
        "wo": pltpu.VMEM((width, width), BF16),
        "ring_gate": pltpu.VMEM((depth, CHUNK, width), BF16),
        "ring_up": pltpu.VMEM((depth, CHUNK, width), BF16),
        "ring_down": pltpu.VMEM((depth, CHUNK, width), BF16),
        "tail_gate": pltpu.VMEM((tail, width), BF16),
        "tail_up": pltpu.VMEM((tail, width), BF16),
        "tail_down": pltpu.VMEM((tail, width), BF16),
        "hidden": pltpu.VMEM((rows_all, padded), BF16),
        "columns": pltpu.VMEM((padded, rows_all), F32),
        "square": pltpu.VMEM((rows_all, CHUNK), F32),
        "turn": pltpu.VMEM((padded // 128 * unit_rows["second"], 128), F32),
        "gain_buf": pltpu.VMEM((2 * bits + 2, 8, width), F32),
    }
    for name in ROWS:
        scratch["row_" + name] = pltpu.VMEM((count, 2, unit_rows[name], rows_all), BF16)
        scratch["peer_" + name] = pltpu.VMEM((count, unit_rows[name], rows_all), BF16)
    for name in COLS:
        scratch["col_" + name] = pltpu.VMEM((2, rows_all, widths[name]), BF16)
    for name, ((row, col), *_) in MATRICES.items():
        shape = (unit_rows[row], widths[col])
        scratch["send_" + name] = pltpu.VMEM((half,) + shape, BF16)
        for level in range(bits):
            scratch[f"land_{name}{level}"] = pltpu.VMEM((half >> level,) + shape, BF16)
    copies = {"pair": (len(ROWS) + len(COLS),), "halo": (2,), "step": (len(NAMES), count), "gain": (bits + 1,)}
    scratch["local_sem"] = pltpu.SemaphoreType.DMA((6,))
    scratch["ring_sem"] = pltpu.SemaphoreType.DMA((3, 2 * (hidden_width // CHUNK + depth)))
    for name, shape in copies.items():
        scratch[name + "_send"] = pltpu.SemaphoreType.DMA(shape)
        scratch[name + "_recv"] = pltpu.SemaphoreType.DMA(shape)

    sizes = (micro, block, width, hidden_width, devices, groups)
    results = pl.pallas_call(
        functools.partial(layer_kernel, sizes, tuple(inputs), tuple(outs), tuple(scratch)),
        out_shape=[jax.ShapeDtypeStruct(*spec) for spec in outs.values()],
        in_specs=in_specs,
        out_specs=[vmem_spec] * len(outs),
        scratch_shapes=list(scratch.values()),
        compiler_params=pltpu.CompilerParams(
            collective_id=0, has_side_effects=True, vmem_limit_bytes=63 * 2**20
        ),
        name="layer",
    )(*inputs.values())
    return dict(zip(outs, handed_on(results)))


def hand_on_kernel(count, *refs):
    sources, targets, passing = (refs[part * count : (part + 1) * count] for part in range(3))
    sems = refs[-1]
    arriving = [
        pltpu.make_async_copy(source, middle, sems.at[0, index])
        for index, (source, middle) in enumerate(zip(sources, passing))
    ]
    leaving = [
        pltpu.make_async_copy(middle, target, sems.at[1, index])
        for index, (middle, target) in enumerate(zip(passing, targets))
    ]
    for copy in arriving:
        copy.start()
    for before, copy in zip(arriving, leaving):
        before.wait()
        copy.start()
    for copy in leaving:
        copy.wait()


def handed_on(arrays):
    any_spec = pl.BlockSpec(memory_space=pl.ANY)
    count = len(arrays)
    return pl.pallas_call(
        functools.partial(hand_on_kernel, count),
        out_shape=[jax.ShapeDtypeStruct(array.shape, array.dtype) for array in arrays],
        in_specs=[any_spec] * count,
        out_specs=[any_spec] * count,
        scratch_shapes=[pltpu.VMEM(array.shape, array.dtype) for array in arrays]
        + [pltpu.SemaphoreType.DMA((2, count))],
        name="hand_on",
    )(*arrays)


def per_device(
    tokens, gain_attn, gain_mlp, w_query, w_key, w_value, w_out, w_gate, w_up, w_down, cotangent, lengths
):
    devices = lax.axis_size("seq")
    groups = min(devices, MOST_GROUPS)
    lower = devices // groups
    micro, block, width = tokens.shape
    weights = dict(
        w_query=w_query, w_key=w_key, w_value=w_value, w_out=w_out, w_gate=w_gate.T, w_up=w_up.T, w_down=w_down
    )
    result = layer(
        tokens.reshape(micro * block, width), gain_attn, gain_mlp, weights,
        cotangent.reshape(micro * block, width), lengths, micro, devices, groups,
    )
    near = [[high * lower + low for low in range(lower)] for high in range(groups)]

    def slice_of(name):
        flat = result["flat_" + name].reshape(-1)
        if lower == 1:
            return flat
        return lax.psum_scatter(flat, "seq", axis_index_groups=near, tiled=True)

    gain_sums = [result["gain_attn_sum"].reshape(-1), result["gain_mlp_sum"].reshape(-1)]
    if lower > 1:
        gain_sums = lax.psum(gain_sums, "seq", axis_index_groups=near)
    return (
        result["output"].reshape(tokens.shape),
        result["input_grad"].reshape(tokens.shape),
        gain_sums[0],
        gain_sums[1],
        slice_of("query"),
        slice_of("keyval"),
        slice_of("value"),
        slice_of("out"),
        slice_of("gate"),
        slice_of("up"),
        slice_of("down"),
    )


def solution(mesh):
    tokens_spec = P(None, "seq", None)
    return jax.shard_map(
        per_device,
        mesh=mesh,
        in_specs=(tokens_spec,) + (P(),) * 9 + (tokens_spec, P()),
        out_specs=(tokens_spec, tokens_spec, P(), P()) + (P("seq"),) * 7,
        check_vma=False,
    )
```

time: 335 us -> 171 us (0.51); the launches traced: 331 us -> 170 us
  local copies, waits for them, and re-layouts: 111 us -> 0 us
  matrix products: 58.4 us -> 0 us
  Pallas kernels: 136 us -> 170 us
  other arithmetic: 14.3 us -> 0 us
  starting transfers between devices: 9.6 us -> 0 us
    dot_general x19 -> x0, matrix products: 56 us -> none  [the longest x7 13.9 us: times_transpose(): lax.dot_general(left, weight, (((1,), (1,)), ((), ())), preferred_element...]
    reshape x16 -> x0, local copies, waits for them, and re-layouts: 36.5 us -> none  [the longest x2 11.4 us: halves(): both = both.reshape(micro, 2, block, width)]
    pallas_call x1 -> x2, Pallas kernels: 136 us -> 170 us  [the longest x1 167 us: layer(): pl.pallas_call(functools.partial(layer_kernel, sizes, tuple(inputs), tupl...]
    unnamed x89 -> x0, local copies, waits for them, and re-layouts: 31.8 us -> none
    slice x8 -> x0, local copies, waits for them, and re-layouts: 19.9 us -> none  [the longest x2 11.8 us: halves(): both[:, 1].reshape(rows_all, width)]
    ppermute x4 -> x0, starting transfers between devices: 9.6 us -> none  [shifted(): lax.ppermute(value, 'seq', [(source, source + steps) for source in range(...]
    dot_general x2 -> x0, local copies, waits for them, and re-layouts: 6.9 us -> none  [the longest x1 3.54 us: per_device(): up = jnp.dot(second, w_up, preferred_element_type=F32)]
    convert_element_type x4 -> x0, local copies, waits for them, and re-layouts: 6.56 us -> none  [the longest x2 3.86 us: per_device(): dquery = dquery.reshape(rows_all, width).astype(BF16)]
  transfers between devices with their start and end apart: 4 -> 0, of which waited for: 0 -> 0; matrix products, arithmetic and copies ran while one was open for 11% -> 0% of each run, Pallas kernels for 0% -> 0%
where the time goes in v2:
time: 171 us; the launch traced here: 170 us
  Pallas kernels  170 us (99%)
    pallas_call x1, Pallas kernels, layer(): pl.pallas_call(functools.partial(layer_kernel, sizes, tuple(inputs), tupl...  167 us

profile of v2, /device:TPU:0, one launch (start us, length us, event | category | flops | bytes accessed | tf_op | source)
XLA Modules:
  0.0 170.5 jit_solution(7399141517448361884)
XLA Ops:
  0.6 166.6 %layer.1 = (bf16[256,1024]{1,0:T(8,128)(2,1)}, f32[256,1024]{1,0:T(8,128)}, f32[8,128]{1,0:T(8,128)}, f32[8,128]{1,0:T(8,128)}, f32[256,128]{1,0:T(8,128)}, /*in...) custom-call(bf16[256,1024]{1,0:T(8,128)(2,1)} %bitcast.19, ...), custom_call_target="tpu_custom_call" | custom-call | tf_op jit(solution)/shard_map/layer/pallas_call | solution.py:702
  167.2 3.1 %hand_on.1 = (bf16[256,1024]{1,0:T(8,128)(2,1)}, f32[256,1024]{1,0:T(8,128)}, f32[8,128]{1,0:T(8,128)}, f32[8,128]{1,0:T(8,128)}, f32[256,128]{1,0:T(8,128)}, /*...) custom-call(bf16[256,1024]{1,0:T(8,128)(2,1)} %get-tuple-element.33., ...), custom_call_target="tpu_custom_call" | custom-call | tf_op jit(solution)/shard_map/hand_on/pallas_call | solution.py:739

commit v3 on v2

--- a/solution.py
+++ b/solution.py
@@ -26,27 +26,148 @@
     "out": (("attended", "branch"),),
 }
 ROWS = ("first", "before", "attended", "second", "hidden")
+CHUNKED = ("dgate", "dup")
 COLS = ("cot", "dgate", "dup", "branch", "dquery", "dkeyval", "dkvback")
-NAMES = tuple(MATRICES)
-INDEX = {name: index for index, name in enumerate(NAMES)}
+PARTS = {
+    "gate": ("gate", 0, 11, "ascending"),
+    "up": ("up", 0, 11, "swapped"),
+    "down": ("down", 0, 3, "last_first"),
+    "rest": ("down", 3, 4, "ascending"),
+    "out": ("out", 0, 4, "ascending"),
+    "query": ("query", 0, 4, "ascending"),
+    "keyval": ("keyval", 0, 8, "swapped"),
+}
+INDEX = {name: index for index, name in enumerate(PARTS)}
+SPANS = (1, 2, 4, 4)
+LAG = 2
+
+
+SCHEDULE = {
+    "middle": (
+        ("gate", 0, 0),
+        ("gate", 0, 2),
+    ),
+    "attend0": (
+        ("gate", 0, 4),
+        ("down", 0, 0),
+        ("up", 0, 0),
+        ("gate", 0, 6),
+    ),
+    "attend1": (
+        ("down", 0, 1),
+        ("up", 0, 2),
+        ("gate", 0, 8),
+        ("up", 0, 4),
+        ("gate", 0, 10),
+        ("up", 0, 6),
+    ),
+    "attend2": (
+        ("up", 0, 8),
+        ("gate", 1, 0),
+        ("down", 0, 2),
+    ),
+    "attend3": (
+        ("rest", 0, 0),
+        ("down", 1, 0),
+        ("up", 0, 10),
+        ("gate", 1, 4),
+    ),
+    "back": (
+        ("up", 1, 0),
+    ),
+    "query": (
+        ("gate", 1, 8),
+    ),
+    "keyval": (
+        ("gate", 2, 0),
+    ),
+    "first": (
+        ("up", 1, 4),
+        ("rest", 1, 0),
+    ),
+    "input": (
+        ("gate", 2, 4),
+        ("up", 1, 8),
+        ("down", 2, 0),
+        ("down", 1, 1),
+        ("down", 1, 2),
+        ("keyval", 0, 0),
+    ),
+    "gain0": (
+        ("up", 2, 0),
+        ("gate", 2, 8),
+        ("gate", 3, 0),
+        ("out", 0, 0),
+    ),
+    "gain1": (
+        ("keyval", 0, 2),
+        ("up", 2, 4),
+    ),
+    "gain2": (
+        ("rest", 2, 0),
+        ("keyval", 0, 4),
+        ("out", 0, 2),
+        ("gate", 3, 4),
+    ),
+    "gain3": (
+        ("up", 2, 8),
+        ("up", 3, 0),
+        ("gate", 3, 8),
+        ("keyval", 0, 6),
+        ("query", 0, 0),
+        ("up", 3, 4),
+        ("down", 3, 0),
+        ("rest", 3, 0),
+        ("up", 3, 8),
+        ("query", 0, 2),
+        ("out", 1, 0),
+        ("down", 2, 1),
+        ("down", 2, 2),
+        ("query", 1, 0),
+        ("out", 2, 0),
+        ("down", 3, 1),
+        ("down", 3, 2),
+        ("keyval", 1, 0),
+        ("query", 2, 0),
+        ("out", 3, 0),
+        ("keyval", 1, 4),
+        ("keyval", 2, 0),
+        ("query", 3, 0),
+        ("keyval", 2, 4),
+        ("keyval", 3, 0),
+        ("keyval", 3, 4),
+    ),
+}
 
 
 def round_up(value, unit):
     return -(-value // unit) * unit
 
 
-def bit_orders(bits):
+def bit_order(kind, bits):
     ascending = list(range(1, bits + 1))
-    swapped = [2, 1] + ascending[2:]
-    last_first = ascending[2:] + [1, 2]
-    return {
-        "down": last_first,
-        "gate": ascending,
-        "query": ascending,
-        "out": ascending,
-        "up": swapped,
-        "keyval": swapped,
-    }
+    if kind == "swapped":
+        return [2, 1] + ascending[2:]
+    if kind == "last_first":
+        return ascending[2:] + [1, 2]
+    return ascending
+
+
+def length(name):
+    return PARTS[name][2] - PARTS[name][1]
+
+
+def step_span(name, level):
+    return 1 if PARTS[name][0] == "down" else SPANS[min(level, len(SPANS) - 1)]
+
+
+def step_layout(bits):
+    places, total = {}, 0
+    for name in PARTS:
+        for level in range(bits):
+            places[name, level] = total
+            total += -(-length(name) // step_span(name, level))
+    return places, total
 
 
 def bit_of(number, bit):
@@ -88,7 +209,8 @@
     bits = groups.bit_length() - 2
     count = 1 << bits
     half = count // 2
-    orders = bit_orders(bits)
+    step_places, _ = step_layout(bits)
+    orders = {name: bit_order(kind, bits) for name, (_, _, _, kind) in PARTS.items()}
     rows_all = micro * block
     chunks = width // CHUNK
     full = hidden_width // CHUNK
@@ -96,6 +218,14 @@
     depth = r["ring_gate"].shape[0]
     kept = full - depth
     scale = 1.0 / math.sqrt(HEAD)
+
+    schedule = SCHEDULE
+    if bits != 4:
+        schedule = {"last": [
+            (name, level, first)
+            for level in range(bits) for name in PARTS
+            for first in range(0, length(name), step_span(name, min(level + 1, bits - 1)))
+        ]}
 
     position = lax.axis_index("seq")
     me, rest = position // lower, position % lower
@@ -127,33 +257,25 @@
         local_copy(r[name].at[past, :], r["tail_" + name[2:]], 3 + index)
         for index, name in enumerate(("w_gate", "w_up", "w_down"))
     ]
-    def attention_weights(base):
-        return [
-            pltpu.make_async_copy(
-                r[name].at[at_chunk(slot), :], r[ring].at[slot], r["ring_sem"].at[index, base + slot]
-            )
-            for index, (name, ring) in enumerate(zip(("w_query", "w_key", "w_value"), rings))
-            for slot in range(depth)
-        ]
-
-    attention_first = attention_weights(2 * full)
-    attention_again = attention_weights(2 * full + depth)
+    attention_weights = [
+        pltpu.make_async_copy(r[name].at[at_chunk(slot), :], r[ring].at[slot], r["ring_sem"].at[index, slot])
+        for index, (name, ring) in enumerate(zip(("w_query", "w_key", "w_value"), rings))
+        for slot in range(depth)
+    ]
 
     def hidden_weights(chunk, place):
         slot = place % depth
         return [
-            pltpu.make_async_copy(r[name].at[at_chunk(chunk), :], r[ring].at[slot], r["ring_sem"].at[index, place])
+            pltpu.make_async_copy(r[name].at[at_chunk(chunk), :], r[ring].at[slot], r["ring_sem"].at[index, slot])
             for index, (name, ring) in enumerate(zip(("w_gate", "w_up", "w_down"), rings))
         ]
-
-    padded = r["col_dgate"].shape[2]
 
     def pair_copies():
         plan = {}
         for name in ROWS:
             plan[name] = (r["row_" + name].at[:, 1 - core], r["peer_" + name])
         plan["cot"] = (r["cotangent"], r["col_cot"].at[1])
-        for name in ("dgate", "dup", "branch", "dquery", "dkeyval", "dkvback"):
+        for name in ("branch", "dquery", "dkeyval", "dkvback"):
             plan[name] = (r["col_" + name].at[0], r["col_" + name].at[1])
         return {
             name: remote_copy(source, target, "pair", index, partner(0))
@@ -164,30 +286,31 @@
     ready = set()
 
     def need(name):
-        if name not in ready:
+        if name not in ready and name not in CHUNKED:
             ready.add(name)
             pair[name].wait_recv()
 
-    halo_out = remote_copy(r["tokens"], r["x_before"], "halo", 0, after)
+    def pair_chunk(first, last=None):
+        ref = r["col_hidden"]
+        some = pl.ds(first, 1 if last is None else last - first)
+        return pltpu.make_async_remote_copy(
+            src_ref=ref.at[0, some], dst_ref=ref.at[1, some],
+            send_sem=r["chunk_send"].at[0], recv_sem=r["chunk_recv"].at[first],
+            device_id=partner(0), device_id_type=MESH,
+        )
+
+    halo_out = remote_copy(r["x"], r["x_before"], "halo", 0, after)
     halo_back = remote_copy(r["back_out"], r["back_in"], "halo", 1, behind)
 
     load_tokens.start()
-    for copy in attention_first:
-        copy.start()
-    load_out.start()
-    load_cot.start()
-    for copy in load_tails:
-        copy.start()
+    r["x_before"][...] = jnp.zeros_like(r["x_before"])
     barrier = pltpu.get_barrier_semaphore()
     for device in [after, behind] + [partner(bit) for bit in range(bits + 1)]:
         pl.semaphore_signal(barrier, inc=1, device_id=device, device_id_type=MESH)
-    pl.semaphore_wait(barrier, bits + 3)
-    halo_out.start()
-    pair["cot"].start()
-    for name in ("dgate", "dup"):
-        r["col_" + name][0, :, pl.ds(full * CHUNK, padded - full * CHUNK)] = jnp.zeros(
-            (rows_all, padded - full * CHUNK), BF16
-        )
+    for copy in attention_weights:
+        copy.start()
+    for part in range(2):
+        r["col_hidden"][0, full, part] = jnp.zeros((rows_all, CHUNK), BF16)
 
 
     def unit_at(order, slot):
@@ -197,56 +320,86 @@
             unit = unit + (1 << (bit - 1)) * rel * (1 - 2 * bit_of(me, bit))
         return unit
 
-    def product(name, first, last, store):
-        units = [unit_at(orders[name], slot) for slot in range(first, last)]
+    def factors(name, base):
+        matrix = PARTS[name][0]
+        units = [unit_at(orders[name], base + slot) for slot in range(half)]
         pairs = []
-        for row, col in MATRICES[name]:
+        for row, col in MATRICES[matrix]:
             need(row)
             need(col)
             for source in range(2):
                 parts = [
                     r["row_" + row][unit, core] if source == 0 else r["peer_" + row][unit] for unit in units
                 ]
-                pairs.append((jnp.concatenate(parts, axis=0), r["col_" + col], source))
-        unit_rows = r["row_" + MATRICES[name][0][0]].shape[2]
-
-        def body(at):
-            lanes = at_chunk(at)
-            total = None
-            for left, ref, source in pairs:
-                term = dot(left, ref[source, :, lanes])
-                total = term if total is None else total + term
-            store(lanes, total.reshape(last - first, unit_rows, CHUNK))
-
-        loop(0, pairs[0][1].shape[2] // CHUNK, body)
-
-    def step_copy(name, level, slot):
+                pairs.append((jnp.concatenate(parts, axis=0), col, source))
+        return pairs
+
+    def product(pairs, chunk):
+        total = None
+        for left, col, source in pairs:
+            if col in CHUNKED:
+                right = r["col_hidden"][source, chunk, CHUNKED.index(col)]
+            else:
+                right = r["col_" + col][source, :, at_chunk(chunk)]
+            term = dot(left, right)
+            total = term if total is None else total + term
+        return total.reshape(half, total.shape[0] // half, CHUNK)
+
+    def step_copy(name, level, first, last):
         size = half >> level
-        source = r["send_" + name].at[slot] if level == 0 else r[f"land_{name}{level - 1}"].at[size + slot]
-        return remote_copy(
-            source, r[f"land_{name}{level}"].at[slot], "step", (INDEX[name], count - 2 * size + slot),
-            partner(orders[name][level]),
+        some = pl.ds(first, last - first)
+        if level == 0:
+            source = r["send_" + name].at[some]
+        else:
+            source = r[f"land_{name}{level - 1}"].at[some, pl.ds(size, size)]
+        place = step_places[name, level] + first // step_span(name, level)
+        return pltpu.make_async_remote_copy(
+            src_ref=source, dst_ref=r[f"land_{name}{level}"].at[some],
+            send_sem=r["step_send"].at[INDEX[name], level], recv_sem=r["step_recv"].at[place],
+            device_id=partner(orders[name][level]), device_id_type=MESH,
         )
 
-    def send_product(name):
-        target = r["send_" + name]
-
-        def store(lanes, value):
-            target[:, :, lanes] = value.astype(BF16)
-
-        product(name, half, count, store)
-        loop(0, half, lambda at: step_copy(name, 0, (at + half // 2) % half).start())
-
-    def finish(name, total):
-        flat = r["flat_" + name]
+    def send_products(name):
+        pairs = factors(name, half)
+        for at in range(length(name)):
+            r["send_" + name][at] = product(pairs, PARTS[name][1] + at).astype(BF16)
+            step_copy(name, 0, at, at + 1).start()
+
+    def arrive(name, level, first):
+        last = min(first + step_span(name, min(level + 1, bits - 1)), length(name))
+        here = r[f"land_{name}{level}"]
+        pairs = factors(name, 0) if level == 0 else None
+        size = half >> level
+        span = step_span(name, level)
+        for at in range(first, last, span):
+            step_copy(name, level, at, min(at + span, last)).wait_recv()
+        for at in range(first, last):
+            if level == 0:
+                own = product(pairs, PARTS[name][1] + at)
+            else:
+                own = r[f"land_{name}{level - 1}"][at, :size].astype(F32)
+            total = own + here[at].astype(F32)
+            if level < bits - 1:
+                here[at] = total.astype(BF16)
+            elif name in ("gate", "up"):
+                rows = total.shape[1]
+                for part in range(CHUNK // 128):
+                    place = (at * (CHUNK // 128) + part) * rows
+                    r["turn_" + name][pl.ds(place, rows), :] = total[0, :, 128 * part : 128 * (part + 1)]
+            else:
+                r["total_" + name][at] = total[0]
+        if level < bits - 1:
+            step_copy(name, level + 1, first, last).start()
+        elif last == length(name):
+            finish(name)
+
+    def finish(name):
         if name in ("gate", "up"):
-            rows, wide = total.shape
-            turn = r["turn"]
-            for j in range(wide // 128):
-                turn[pl.ds(rows * j, rows), :] = total[:, 128 * j : 128 * (j + 1)]
+            flat, turn = r["flat_" + name], r["turn_" + name]
+            whole = hidden_width // 128
+            steps = hidden_width // 64
+            rows = turn.shape[0] // (whole + 1)
             few = rows // 2
-            steps = hidden_width // 64
-            whole = hidden_width // 128
             even = [turn[pl.ds(rows * j, few, stride=2), :] for j in range(whole + 1)]
             odd = [pltpu.roll(turn[pl.ds(rows * j + 1, few, stride=2), :], 64, 1) for j in range(whole + 1)]
             low = lax.broadcasted_iota(jnp.int32, (few, 128), 1) < 64
@@ -255,41 +408,15 @@
                 flat[pl.ds(whole + 1 + j, few, stride=steps), :] = jnp.where(low, odd[j], odd[j + 1])
             flat[pl.ds(whole, few, stride=steps), :] = jnp.where(low, even[whole], odd[0])
             return
-        parts = ((flat, 0),)
-        if name == "keyval":
-            parts = ((flat, 0), (r["flat_value"], width))
+        matrix, first, last, _ = PARTS[name]
         per_row = width // 128
-        for ref, base in parts:
-            rows = ref.shape[0] // per_row
-            for j in range(per_row):
-                ref[pl.ds(j, rows, stride=per_row), :] = total[:rows, base + 128 * j : base + 128 * (j + 1)]
-
-    def arrive(name, level, first, last, forward):
-        size = half >> level
-        buffer = r[f"land_{name}{level}"]
-        if level == 0:
-            loop(first, last, lambda slot: step_copy(name, 0, slot).wait_recv())
-
-            def store(lanes, value):
-                buffer[first:last, :, lanes] = (value + buffer[first:last, :, lanes].astype(F32)).astype(BF16)
-
-            product(name, first, last, store)
-            if forward:
-                loop(first, last, lambda slot: step_copy(name, 1, slot - size // 2).start())
-            return
-        before = r[f"land_{name}{level - 1}"]
-
-        def body(slot):
-            step_copy(name, level, slot).wait_recv()
-            total = buffer[slot].astype(F32) + before[slot].astype(F32)
-            if level == bits - 1:
-                finish(name, total)
-            else:
-                buffer[slot] = total.astype(BF16)
-            if forward:
-                step_copy(name, level + 1, slot - size // 2).start()
-
-        loop(first, last, body)
+        for at in range(last - first):
+            total = r["total_" + name][at]
+            for part in range(CHUNK // 128):
+                column = (first + at) * (CHUNK // 128) + part
+                target = "flat_value" if column >= per_row else "flat_" + matrix
+                rows = r[target].shape[0] // per_row
+                r[target][pl.ds(column % per_row, rows, stride=per_row), :] = total[:rows, 128 * part : 128 * (part + 1)]
 
     def gain_copy(bit):
         return remote_copy(r["gain_buf"].at[2 * bit], r["gain_buf"].at[2 * bit + 1], "gain", bit, partner(bit))
@@ -305,6 +432,10 @@
                 for j in range(width // 128):
                     r[name][j : j + 1, :] = total[row : row + 1, 128 * j : 128 * (j + 1)]
 
+    def arrivals(point):
+        for name, level, first in schedule.get(point, ()):
+            arrive(name, level, first)
+
 
     def some_rows(at):
         return pl.ds(at * block, block)
@@ -325,25 +456,23 @@
         pair[name].start()
 
     def project(left, ring, target):
-        def body(at):
-            total = dot(left[:, at_chunk(0)], r[ring][0, :, at_chunk(at)])
-            for part in range(1, chunks):
-                total += dot(left[:, at_chunk(part)], r[ring][part, :, at_chunk(at)])
-            target[:, at_chunk(at)] = total.astype(BF16)
-
-        loop(0, chunks, body)
+        target[...] = dot(left[...], r[ring][...].reshape(width, width)).astype(BF16)
 
     act, other = r["act"], r["other"]
     load_tokens.wait()
+    pl.semaphore_wait(barrier, bits + 3)
+    pl.when(position < devices - 1)(halo_out.start)
     first_norm(r["x"], act)
-    by_owner("first", act)
+    load_out.start()
+    load_cot.start()
+    for copy in load_tails:
+        copy.start()
     for index, (ring, target) in enumerate(zip(rings, ("queries", "keys", "values"))):
-        for copy in attention_first[index * depth : (index + 1) * depth]:
+        for copy in attention_weights[index * depth : (index + 1) * depth]:
             copy.wait()
         project(act, ring, r[target])
-    halo_out.wait_recv()
+    pl.when(position > 0)(halo_out.wait_recv)
     first_norm(r["x_before"], other)
-    by_owner("before", other)
     project(other, "ring_up", r["keys_before"])
     project(other, "ring_down", r["values_before"])
     for slot in range(depth):
@@ -397,16 +526,12 @@
         mixed = dot_cols(probability, both("values_before", "values", rows, lanes))
         act[rows, lanes] = unstacked(mixed).astype(BF16)
 
-    loop(0, micro * chunks, attend)
-    by_owner("attended", act)
+    pair["cot"].start()
+    loop(0, micro * chunks, attend, unroll=2)
     load_out.wait()
     middle = r["input_grad"]
 
-    def out_project(at):
-        lanes = at_chunk(at)
-        middle[:, lanes] = r["x"][:, lanes].astype(F32) + dot(act[...], r["wo"][:, lanes])
-
-    loop(0, chunks, out_project)
+    middle[...] = r["x"][...].astype(F32) + dot(act[...], r["wo"][...])
 
     def second_norm(at):
         value = middle[some_rows(at), :]
@@ -429,19 +554,42 @@
         slot = at % depth
         for copy in hidden_weights(at, at):
             copy.wait()
+        wait_chunk(at - LAG)
         hidden, dgate, dup = hidden_part(
             dot_rows(other[...], r["ring_gate"][slot]),
             dot_rows(other[...], r["ring_up"][slot]),
             dot_rows(r["col_cot"][0], r["ring_down"][slot]),
         )
         lanes = at_chunk(at)
+        form_chunk(at - LAG)
         r["hidden"][:, lanes] = hidden
-        r["col_dgate"][0, :, lanes] = dgate
-        r["col_dup"][0, :, lanes] = dup
+        r["col_hidden"][0, at, 0] = dgate
+        r["col_hidden"][0, at, 1] = dup
         columns[lanes, :] = hidden.astype(F32).T
+        pair_chunk(at).start()
+        send_chunk(at - LAG)
         if prefetch:
             for copy in hidden_weights(at + depth, at + depth):
                 copy.start()
+
+    early = (("gate", "dgate"), ("up", "dup"))
+    early_factors = {}
+
+    def wait_chunk(at):
+        if at >= 0:
+            pair_chunk(at).wait_recv()
+
+    def form_chunk(at):
+        if at >= 0:
+            for name, _ in early:
+                if name not in early_factors:
+                    early_factors[name] = factors(name, half)
+                r["send_" + name][at] = product(early_factors[name], at).astype(BF16)
+
+    def send_chunk(at):
+        if at >= 0:
+            for name, _ in early:
+                step_copy(name, 0, at, at + 1).start()
 
     load_cot.wait()
     for copy in load_tails:
@@ -454,8 +602,9 @@
         dot_rows(r["col_cot"][0], r["tail_down"][...]),
     )
     r["hidden"][:, past] = hidden
-    r["col_dgate"][0, :, past] = dgate
-    r["col_dup"][0, :, past] = dup
+    r["col_hidden"][0, full, 0, :, :tail] = dgate
+    r["col_hidden"][0, full, 1, :, :tail] = dup
+    pair_chunk(full).start()
     r["square"][...] = jnp.zeros_like(r["square"])
     r["square"][:, :tail] = hidden.astype(F32)
     columns[pl.ds(full * CHUNK, CHUNK), :] = r["square"][...].T
@@ -464,46 +613,52 @@
     for owner in range(groups):
         r["row_hidden"][owner // 2, owner % 2] = columns[pl.ds(owner * own_rows, held_rows), :].astype(BF16)
     pair["hidden"].start()
-    pair["dgate"].start()
-    pair["dup"].start()
-    send_product("down")
-    send_product("gate")
-    send_product("up")
+    for at in range(full - LAG, full + 1):
+        wait_chunk(at)
+        form_chunk(at)
+        send_chunk(at)
+    send_products("down")
+    send_products("rest")
 
 
     sums = [pl.ds(n * CHUNK, CHUNK) for n in range(2 * chunks)]
 
-    def fold(hidden, dgate, dup, gate_ref, up_ref, down_ref):
-        back = dot(dgate, gate_ref[...]) + dot(dup, up_ref[...])
-        onward = dot(hidden, down_ref[...])
+    def fold(*pieces):
+        back, onward = None, None
+        for hidden, dgate, dup, gate_ref, up_ref, down_ref in pieces:
+            one = dot(dgate, gate_ref[...]) + dot(dup, up_ref[...])
+            two = dot(hidden, down_ref[...])
+            back, onward = (one, two) if back is None else (back + one, onward + two)
         for n in range(chunks):
             columns[sums[n], :] += back[:, n * CHUNK : (n + 1) * CHUNK]
             columns[sums[chunks + n], :] += onward[:, n * CHUNK : (n + 1) * CHUNK]
 
-    def fold_chunk(at, arrived, prefetch):
-        slot = at % depth
-        chunk = at - depth if arrived else at - depth - full
-        if not arrived:
-            for copy in hidden_weights(chunk, at):
-                copy.wait()
-        lanes = at_chunk(chunk)
-        fold(
-            r["hidden"][:, lanes], r["col_dgate"][0, :, lanes], r["col_dup"][0, :, lanes],
-            *(r[ring].at[slot] for ring in rings),
-        )
-        if prefetch:
-            for copy in hidden_weights(at - full, at + depth):
-                copy.start()
+    def fold_chunks(places):
+        pieces = []
+        for at in places:
+            chunk = at - depth if at < full + depth else at - depth - full
+            if at >= full + depth:
+                for copy in hidden_weights(chunk, at):
+                    copy.wait()
+            pieces.append((
+                r["hidden"][:, at_chunk(chunk)], r["col_hidden"][0, chunk, 0], r["col_hidden"][0, chunk, 1],
+                *(r[ring].at[at % depth] for ring in rings),
+            ))
+        fold(*pieces)
+        for at in places:
+            if at < full + kept:
+                for copy in hidden_weights(at - full, at + depth):
+                    copy.start()
 
     for some in sums:
         columns[some, :] = jnp.zeros((CHUNK, CHUNK), F32)
-    fold(
-        r["hidden"][:, past], r["col_dgate"][0, :, past], r["col_dup"][0, :, past],
+    fold((
+        r["hidden"][:, past], r["col_hidden"][0, full, 0, :, :tail], r["col_hidden"][0, full, 1, :, :tail],
         r["tail_gate"], r["tail_up"], r["tail_down"],
-    )
-    for at in range(full, 2 * full):
-        fold_chunk(at, at < full + depth, at < full + kept)
-    for copy in attention_again:
+    ))
+    for at in range(full, 2 * full, 2):
+        fold_chunks(range(at, min(at + 2, 2 * full)))
+    for copy in attention_weights:
         copy.start()
 
     def summed(at, base):
@@ -531,11 +686,12 @@
 
     gain_mlp_sum = lax.fori_loop(0, micro, middle_backward, jnp.zeros((1, width), F32))
     pair["branch"].start()
-
-    def attended_backward(at):
-        r["grad_attended"][:, at_chunk(at)] = dot_rows(r["col_branch"][0], r["wo"][at_chunk(at), :]).astype(BF16)
-
-    loop(0, chunks, attended_backward)
+    by_owner("attended", act)
+    for name, source in (("first", "x"), ("before", "x_before")):
+        first_norm(r[source], r["back_out"])
+        by_owner(name, r["back_out"])
+
+    r["grad_attended"][...] = dot_rows(r["col_branch"][0], r["wo"][...]).astype(BF16)
 
 
     def attend_backward(index):
@@ -557,10 +713,14 @@
         r["col_dkeyval"][0, rows, lanes] = dkey[block:]
         r["col_dkeyval"][0, rows, lanes_value] = dvalue[block:]
 
-    loop(0, micro * chunks, attend_backward)
+    arrivals("middle")
+    for at in range(micro):
+        loop(at * chunks, (at + 1) * chunks, attend_backward, unroll=2)
+        arrivals("attend" + str(at))
     for name in ("dquery", "dkeyval", "dkvback"):
         pair[name].start()
-    send_product("out")
+    send_products("out")
+    arrivals("out")
 
     def through_keys(ref, at):
         return dot_rows(ref[0, :, :width], r["ring_up"][at]) + dot_rows(ref[0, :, width:], r["ring_down"][at])
@@ -573,13 +733,17 @@
             r["col_dquery"][0], r["ring_gate"][at]
         )
 
-    for copy in attention_again:
+    for copy in attention_weights:
         copy.wait()
     loop(0, chunks, back_chunk)
     pl.when(position > 0)(halo_back.start)
-    send_product("query")
-    send_product("keyval")
+    arrivals("back")
+    send_products("query")
+    arrivals("query")
+    send_products("keyval")
+    arrivals("keyval")
     loop(0, chunks, first_chunk)
+    arrivals("first")
 
 
     def input_backward(at, gain_sum):
@@ -590,35 +754,29 @@
         middle[rows, :] = middle[rows, :] + grad
         return gain_sum + part
 
-    turn = ("gate", "up", "down", "query", "keyval", "out")
-    for level in range(bits):
-        size = half >> level
-        if level > 0:
-            gain_step(level - 1)
-        for name in turn:
-            if size > 1:
-                arrive(name, level, size // 2, size, True)
-        for name in turn:
-            arrive(name, level, 0, max(size // 2, 1), False)
-        if level == 0:
-            pl.when(position < devices - 1)(halo_back.wait_recv)
-            gain_attn_sum = lax.fori_loop(0, micro, input_backward, jnp.zeros((1, width), F32))
-            r["gain_buf"][0] = jnp.concatenate(
-                [gain_attn_sum, gain_mlp_sum, jnp.zeros((6, width), F32)], axis=0
-            )
-            gain_copy(0).start()
+    pl.when(position < devices - 1)(halo_back.wait_recv)
+    gain_attn_sum = lax.fori_loop(0, micro, input_backward, jnp.zeros((1, width), F32))
+    r["gain_buf"][0] = jnp.concatenate([gain_attn_sum, gain_mlp_sum, jnp.zeros((6, width), F32)], axis=0)
+    gain_copy(0).start()
+    arrivals("input")
+    for bit in range(bits - 1):
+        gain_step(bit)
+        arrivals("gain" + str(bit))
     gain_step(bits - 1)
+    arrivals("gain" + str(bits - 1))
     gain_step(bits)
-
-    halo_out.wait_send()
+    arrivals("last")
+
+    pl.when(position < devices - 1)(halo_out.wait_send)
     pl.when(position > 0)(halo_back.wait_send)
     for copy in pair.values():
         copy.wait_send()
     for bit in range(bits + 1):
         gain_copy(bit).wait_send()
-    for name in NAMES:
+    pair_chunk(0, full + 1).wait_send()
+    for name in PARTS:
         for level in range(bits):
-            loop(0, half >> level, lambda slot: step_copy(name, level, slot).wait_send())
+            step_copy(name, level, 0, length(name)).wait_send()
 
 
 def layer(tokens, gain_attn, gain_mlp, weights, cotangent, lengths, micro, devices, groups):
@@ -635,7 +793,7 @@
     unit_rows = {name: width // groups for name in ROWS}
     unit_rows["hidden"] = round_up(hidden_width // groups, 16)
     widths = {name: width for name in COLS}
-    widths.update(dgate=padded, dup=padded, dkeyval=2 * width, dkvback=2 * width)
+    widths.update(dkeyval=2 * width, dkvback=2 * width)
 
     inputs = {"tokens": tokens, "cotangent": cotangent, **weights}
     any_spec = pl.BlockSpec(memory_space=pl.ANY)
@@ -678,25 +836,31 @@
         "hidden": pltpu.VMEM((rows_all, padded), BF16),
         "columns": pltpu.VMEM((padded, rows_all), F32),
         "square": pltpu.VMEM((rows_all, CHUNK), F32),
-        "turn": pltpu.VMEM((padded // 128 * unit_rows["second"], 128), F32),
         "gain_buf": pltpu.VMEM((2 * bits + 2, 8, width), F32),
     }
     for name in ROWS:
         scratch["row_" + name] = pltpu.VMEM((count, 2, unit_rows[name], rows_all), BF16)
         scratch["peer_" + name] = pltpu.VMEM((count, unit_rows[name], rows_all), BF16)
     for name in COLS:
-        scratch["col_" + name] = pltpu.VMEM((2, rows_all, widths[name]), BF16)
-    for name, ((row, col), *_) in MATRICES.items():
-        shape = (unit_rows[row], widths[col])
-        scratch["send_" + name] = pltpu.VMEM((half,) + shape, BF16)
+        if name not in CHUNKED:
+            scratch["col_" + name] = pltpu.VMEM((2, rows_all, widths[name]), BF16)
+    scratch["col_hidden"] = pltpu.VMEM((2, padded // CHUNK, len(CHUNKED), rows_all, CHUNK), BF16)
+    for name, (matrix, first, last, _) in PARTS.items():
+        rows = unit_rows[MATRICES[matrix][0][0]]
+        scratch["send_" + name] = pltpu.VMEM((last - first, half, rows, CHUNK), BF16)
         for level in range(bits):
-            scratch[f"land_{name}{level}"] = pltpu.VMEM((half >> level,) + shape, BF16)
-    copies = {"pair": (len(ROWS) + len(COLS),), "halo": (2,), "step": (len(NAMES), count), "gain": (bits + 1,)}
-    scratch["local_sem"] = pltpu.SemaphoreType.DMA((6,))
-    scratch["ring_sem"] = pltpu.SemaphoreType.DMA((3, 2 * (hidden_width // CHUNK + depth)))
-    for name, shape in copies.items():
-        scratch[name + "_send"] = pltpu.SemaphoreType.DMA(shape)
-        scratch[name + "_recv"] = pltpu.SemaphoreType.DMA(shape)
+            scratch[f"land_{name}{level}"] = pltpu.VMEM((last - first, half >> level, rows, CHUNK), BF16)
+        if name in ("gate", "up"):
+            scratch["turn_" + name] = pltpu.VMEM(((last - first) * CHUNK // 128 * rows, 128), F32)
+        else:
+            scratch["total_" + name] = pltpu.VMEM((last - first, rows, CHUNK), F32)
+    sems = {"local_sem": (6,), "ring_sem": (3, depth)}
+    sems.update(chunk_send=(1,), chunk_recv=(padded // CHUNK,))
+    sems.update(step_send=(len(PARTS), bits), step_recv=(step_layout(bits)[1],))
+    for name, number in (("pair", len(ROWS) + len(COLS) - len(CHUNKED)), ("halo", 2), ("gain", bits + 1)):
+        sems[name + "_send"] = sems[name + "_recv"] = (number,)
+    for name, shape in sems.items():
+        scratch[name] = pltpu.SemaphoreType.DMA(shape)
 
     sizes = (micro, block, width, hidden_width, devices, groups)
     results = pl.pallas_call(

time: 171 us -> 162 us (0.947)
  Pallas kernels: 170 us -> 161 us
    pallas_call x1, Pallas kernels: 167 us -> 158 us  [layer(): pl.pallas_call(functools.partial(layer_kernel, sizes, tuple(inputs), tupl...]
where the time goes in v3:
time: 162 us
  Pallas kernels  161 us (99%)
    pallas_call x1, Pallas kernels, layer(): pl.pallas_call(functools.partial(layer_kernel, sizes, tuple(inputs), tupl...  158 us

profile of v3, /device:TPU:0, one launch (start us, length us, event | category | flops | bytes accessed | tf_op | source)
XLA Modules:
  0.0 161.6 jit_solution(4758833289951781176)
XLA Ops:
  0.6 157.6 %layer.1 = (bf16[256,1024]{1,0:T(8,128)(2,1)}, f32[256,1024]{1,0:T(8,128)}, f32[8,128]{1,0:T(8,128)}, f32[8,128]{1,0:T(8,128)}, f32[256,128]{1,0:T(8,128)}, /*in...) custom-call(bf16[256,1024]{1,0:T(8,128)(2,1)} %bitcast.19, ...), custom_call_target="tpu_custom_call" | custom-call | tf_op jit(solution)/shard_map/layer/pallas_call | solution.py:866
  158.3 3.1 %hand_on.1 = (bf16[256,1024]{1,0:T(8,128)(2,1)}, f32[256,1024]{1,0:T(8,128)}, f32[8,128]{1,0:T(8,128)}, f32[8,128]{1,0:T(8,128)}, f32[256,128]{1,0:T(8,128)}, /*...) custom-call(bf16[256,1024]{1,0:T(8,128)(2,1)} %get-tuple-element.33., ...), custom_call_target="tpu_custom_call" | custom-call | tf_op jit(solution)/shard_map/hand_on/pallas_call | solution.py:903

commit v4 on v3

--- a/solution.py
+++ b/solution.py
@@ -29,113 +29,144 @@
 CHUNKED = ("dgate", "dup")
 COLS = ("cot", "dgate", "dup", "branch", "dquery", "dkeyval", "dkvback")
 PARTS = {
-    "gate": ("gate", 0, 11, "ascending"),
-    "up": ("up", 0, 11, "swapped"),
-    "down": ("down", 0, 3, "last_first"),
-    "rest": ("down", 3, 4, "ascending"),
-    "out": ("out", 0, 4, "ascending"),
-    "query": ("query", 0, 4, "ascending"),
-    "keyval": ("keyval", 0, 8, "swapped"),
+    "gate": ("gate", 0, 4, (2, 1, 4, 3), (1, 2, 4, 4)),
+    "gate2": ("gate", 4, 11, (3, 1, 4, 2), (1, 1, 2, 2)),
+    "up": ("up", 0, 3, (3, 4, 2, 1), (1, 1, 2, 2)),
+    "up2": ("up", 3, 11, (1, 3, 4, 2), (1, 2, 4, 4)),
+    "down": ("down", 0, 3, (2, 1, 4, 3), (1, 1, 1, 1)),
+    "rest": ("down", 3, 4, (2, 1, 4, 3), (1, 1, 1, 1)),
+    "out": ("out", 0, 4, (2, 1, 3, 4), (1, 1, 2, 2)),
+    "query": ("query", 0, 4, (1, 3, 2, 4), (1, 1, 2, 2)),
+    "key": ("keyval", 0, 4, (2, 3, 1, 4), (1, 1, 2, 2)),
+    "keyb": ("keyval", 4, 8, (2, 1, 3, 4), (1, 1, 2, 2)),
 }
 INDEX = {name: index for index, name in enumerate(PARTS)}
-SPANS = (1, 2, 4, 4)
 LAG = 2
 
 
 SCHEDULE = {
     "middle": (
         ("gate", 0, 0),
+        ("up", 0, 0),
         ("gate", 0, 2),
+        ("up", 0, 1),
+        ("up", 0, 2),
+        ("gate2", 0, 0),
+        ("up2", 0, 0),
+        ("gate2", 0, 1),
     ),
     "attend0": (
-        ("gate", 0, 4),
+        ("gate2", 0, 2),
+        ("up2", 0, 2),
+        ("gate2", 0, 3),
+        ("gate2", 0, 4),
+    ),
+    "attend1": (
+        ("gate", 1, 0),
+        ("gate2", 0, 5),
+        ("gate2", 0, 6),
+        ("up2", 0, 4),
         ("down", 0, 0),
-        ("up", 0, 0),
-        ("gate", 0, 6),
-    ),
-    "attend1": (
+    ),
+    "attend2": (
+        ("gate2", 1, 0),
+        ("gate2", 1, 2),
         ("down", 0, 1),
-        ("up", 0, 2),
-        ("gate", 0, 8),
-        ("up", 0, 4),
-        ("gate", 0, 10),
-        ("up", 0, 6),
-    ),
-    "attend2": (
-        ("up", 0, 8),
-        ("gate", 1, 0),
+        ("up", 1, 0),
+        ("up2", 1, 0),
+        ("up", 1, 2),
+    ),
+    "attend3": (
+        ("gate2", 1, 4),
         ("down", 0, 2),
-    ),
-    "attend3": (
+        ("gate2", 1, 6),
+    ),
+    "back": (
+        ("gate", 2, 0),
+        ("up2", 0, 6),
+    ),
+    "first": (
+        ("down", 1, 2),
+        ("up", 2, 0),
+        ("up", 2, 2),
+        ("up2", 1, 4),
         ("rest", 0, 0),
+        ("out", 0, 0),
+        ("out", 0, 1),
+    ),
+    "key": (
         ("down", 1, 0),
-        ("up", 0, 10),
-        ("gate", 1, 4),
-    ),
-    "back": (
-        ("up", 1, 0),
-    ),
-    "query": (
-        ("gate", 1, 8),
-    ),
-    "keyval": (
-        ("gate", 2, 0),
-    ),
-    "first": (
-        ("up", 1, 4),
+    ),
+    "keyb": (
+        ("down", 1, 1),
+    ),
+    "gain0": (
+        ("out", 0, 2),
+        ("gate2", 2, 0),
+        ("gate2", 2, 2),
+        ("gate2", 2, 4),
+        ("query", 0, 0),
+        ("gate2", 2, 6),
+        ("up2", 2, 0),
+        ("out", 0, 3),
+        ("gate", 3, 0),
+        ("query", 0, 1),
+        ("down", 2, 0),
+        ("key", 0, 0),
+        ("query", 0, 2),
+        ("key", 0, 1),
+        ("query", 1, 0),
+        ("down", 2, 1),
+        ("query", 0, 3),
+        ("up", 3, 0),
+        ("up", 3, 2),
+        ("key", 0, 2),
+        ("down", 3, 0),
+        ("down", 2, 2),
+        ("key", 0, 3),
+        ("key", 1, 0),
         ("rest", 1, 0),
-    ),
-    "input": (
-        ("gate", 2, 4),
-        ("up", 1, 8),
-        ("down", 2, 0),
-        ("down", 1, 1),
-        ("down", 1, 2),
-        ("keyval", 0, 0),
-    ),
-    "gain0": (
-        ("up", 2, 0),
-        ("gate", 2, 8),
-        ("gate", 3, 0),
-        ("out", 0, 0),
+        ("down", 3, 1),
+        ("keyb", 0, 0),
+        ("query", 1, 2),
+        ("out", 1, 0),
+        ("up2", 2, 4),
+        ("keyb", 0, 1),
+        ("down", 3, 2),
+        ("out", 1, 2),
+        ("key", 1, 2),
+        ("key", 2, 0),
+        ("keyb", 0, 2),
+        ("out", 2, 0),
+        ("keyb", 1, 0),
+        ("keyb", 0, 3),
+        ("rest", 2, 0),
+        ("out", 2, 2),
+        ("key", 2, 2),
     ),
     "gain1": (
-        ("keyval", 0, 2),
-        ("up", 2, 4),
-    ),
-    "gain2": (
-        ("rest", 2, 0),
-        ("keyval", 0, 4),
-        ("out", 0, 2),
-        ("gate", 3, 4),
-    ),
-    "gain3": (
-        ("up", 2, 8),
-        ("up", 3, 0),
-        ("gate", 3, 8),
-        ("keyval", 0, 6),
-        ("query", 0, 0),
-        ("up", 3, 4),
-        ("down", 3, 0),
+        ("gate2", 3, 0),
+        ("gate2", 3, 2),
+        ("gate2", 3, 4),
+        ("gate2", 3, 6),
+        ("key", 3, 0),
+        ("out", 3, 0),
+        ("up2", 3, 0),
+        ("keyb", 2, 0),
+        ("keyb", 1, 2),
+        ("query", 2, 0),
         ("rest", 3, 0),
-        ("up", 3, 8),
-        ("query", 0, 2),
-        ("out", 1, 0),
-        ("down", 2, 1),
-        ("down", 2, 2),
-        ("query", 1, 0),
-        ("out", 2, 0),
-        ("down", 3, 1),
-        ("down", 3, 2),
-        ("keyval", 1, 0),
-        ("query", 2, 0),
-        ("out", 3, 0),
-        ("keyval", 1, 4),
-        ("keyval", 2, 0),
+        ("query", 2, 2),
+        ("out", 3, 2),
+        ("up2", 3, 4),
+        ("key", 3, 2),
+        ("keyb", 2, 2),
+        ("keyb", 3, 0),
+    ),
+    "last": (
         ("query", 3, 0),
-        ("keyval", 2, 4),
-        ("keyval", 3, 0),
-        ("keyval", 3, 4),
+        ("query", 3, 2),
+        ("keyb", 3, 2),
     ),
 }
 
@@ -144,21 +175,12 @@
     return -(-value // unit) * unit
 
 
-def bit_order(kind, bits):
-    ascending = list(range(1, bits + 1))
-    if kind == "swapped":
-        return [2, 1] + ascending[2:]
-    if kind == "last_first":
-        return ascending[2:] + [1, 2]
-    return ascending
-
-
 def length(name):
     return PARTS[name][2] - PARTS[name][1]
 
 
 def step_span(name, level):
-    return 1 if PARTS[name][0] == "down" else SPANS[min(level, len(SPANS) - 1)]
+    return PARTS[name][4][level]
 
 
 def step_layout(bits):
@@ -168,6 +190,10 @@
             places[name, level] = total
             total += -(-length(name) // step_span(name, level))
     return places, total
+
+
+def stage_copies(bits):
+    return 1 + (1 << min(bits, 2)) - 1 + (1 << max(bits - 2, 0)) - 1
 
 
 def bit_of(number, bit):
@@ -210,7 +236,7 @@
     count = 1 << bits
     half = count // 2
     step_places, _ = step_layout(bits)
-    orders = {name: bit_order(kind, bits) for name, (_, _, _, kind) in PARTS.items()}
+    orders = {name: [bit for bit in part[3] if bit <= bits] for name, part in PARTS.items()}
     rows_all = micro * block
     chunks = width // CHUNK
     full = hidden_width // CHUNK
@@ -234,8 +260,18 @@
     after = ((position + 1) % devices,)
     behind = ((position + devices - 1) % devices,)
 
-    def partner(bit):
-        return (flip(me, bit) * lower + rest,)
+    def partner(*some):
+        other = me
+        for bit in some:
+            other = flip(other, bit)
+        return (other * lower + rest,)
+
+    stages = [[0], list(range(1, bits + 1))[:2], list(range(1, bits + 1))[2:]]
+    stages = [stage for stage in stages if stage]
+    peers = [
+        [partner(*[bit for place, bit in enumerate(stage) if mask >> place & 1]) for mask in range(1, 1 << len(stage))]
+        for stage in stages
+    ]
 
 
     def local_copy(source, target, index):
@@ -305,7 +341,8 @@
     load_tokens.start()
     r["x_before"][...] = jnp.zeros_like(r["x_before"])
     barrier = pltpu.get_barrier_semaphore()
-    for device in [after, behind] + [partner(bit) for bit in range(bits + 1)]:
+    greeted = [after, behind] + [device for stage in peers for device in stage]
+    for device in greeted:
         pl.semaphore_signal(barrier, inc=1, device_id=device, device_id_type=MESH)
     for copy in attention_weights:
         copy.start()
@@ -367,6 +404,7 @@
 
     def arrive(name, level, first):
         last = min(first + step_span(name, min(level + 1, bits - 1)), length(name))
+        matrix, base = PARTS[name][:2]
         here = r[f"land_{name}{level}"]
         pairs = factors(name, 0) if level == 0 else None
         size = half >> level
@@ -375,27 +413,33 @@
             step_copy(name, level, at, min(at + span, last)).wait_recv()
         for at in range(first, last):
             if level == 0:
-                own = product(pairs, PARTS[name][1] + at)
+                own = product(pairs, base + at)
             else:
                 own = r[f"land_{name}{level - 1}"][at, :size].astype(F32)
             total = own + here[at].astype(F32)
             if level < bits - 1:
                 here[at] = total.astype(BF16)
-            elif name in ("gate", "up"):
+            elif matrix in ("gate", "up"):
                 rows = total.shape[1]
                 for part in range(CHUNK // 128):
-                    place = (at * (CHUNK // 128) + part) * rows
-                    r["turn_" + name][pl.ds(place, rows), :] = total[0, :, 128 * part : 128 * (part + 1)]
+                    place = ((base + at) * (CHUNK // 128) + part) * rows
+                    r["turn_" + matrix][pl.ds(place, rows), :] = total[0, :, 128 * part : 128 * (part + 1)]
             else:
                 r["total_" + name][at] = total[0]
         if level < bits - 1:
             step_copy(name, level + 1, first, last).start()
-        elif last == length(name):
-            finish(name)
-
-    def finish(name):
-        if name in ("gate", "up"):
-            flat, turn = r["flat_" + name], r["turn_" + name]
+        else:
+            unfinished[matrix] -= last - first
+            if not unfinished[matrix]:
+                finish(matrix)
+
+    unfinished = {}
+    for name, part in PARTS.items():
+        unfinished[part[0]] = unfinished.get(part[0], 0) + length(name)
+
+    def finish(matrix):
+        if matrix in ("gate", "up"):
+            flat, turn = r["flat_" + matrix], r["turn_" + matrix]
             whole = hidden_width // 128
             steps = hidden_width // 64
             rows = turn.shape[0] // (whole + 1)
@@ -408,29 +452,41 @@
                 flat[pl.ds(whole + 1 + j, few, stride=steps), :] = jnp.where(low, odd[j], odd[j + 1])
             flat[pl.ds(whole, few, stride=steps), :] = jnp.where(low, even[whole], odd[0])
             return
-        matrix, first, last, _ = PARTS[name]
         per_row = width // 128
-        for at in range(last - first):
-            total = r["total_" + name][at]
-            for part in range(CHUNK // 128):
-                column = (first + at) * (CHUNK // 128) + part
-                target = "flat_value" if column >= per_row else "flat_" + matrix
-                rows = r[target].shape[0] // per_row
-                r[target][pl.ds(column % per_row, rows, stride=per_row), :] = total[:rows, 128 * part : 128 * (part + 1)]
-
-    def gain_copy(bit):
-        return remote_copy(r["gain_buf"].at[2 * bit], r["gain_buf"].at[2 * bit + 1], "gain", bit, partner(bit))
-
-    def gain_step(bit):
-        gain_copy(bit).wait_recv()
-        total = r["gain_buf"][2 * bit] + r["gain_buf"][2 * bit + 1]
-        if bit < bits:
-            r["gain_buf"][2 * bit + 2] = total
-            gain_copy(bit + 1).start()
-        else:
-            for row, name in enumerate(("gain_attn_sum", "gain_mlp_sum")):
-                for j in range(width // 128):
-                    r[name][j : j + 1, :] = total[row : row + 1, 128 * j : 128 * (j + 1)]
+        for name, part in PARTS.items():
+            if part[0] != matrix:
+                continue
+            for at in range(length(name)):
+                total = r["total_" + name][at]
+                for piece in range(CHUNK // 128):
+                    column = (part[1] + at) * (CHUNK // 128) + piece
+                    target = "flat_value" if column >= per_row else "flat_" + matrix
+                    rows = r[target].shape[0] // per_row
+                    r[target][pl.ds(column % per_row, rows, stride=per_row), :] = total[:rows, 128 * piece : 128 * (piece + 1)]
+
+    def gain_copy(stage, index):
+        base = sum(len(group) + 1 for group in peers[:stage])
+        return remote_copy(
+            r["gain_buf"].at[base], r["gain_buf"].at[base + 1 + index], "gain", base - stage + index, peers[stage][index]
+        )
+
+    def gain_start(stage, value):
+        r["gain_buf"][sum(len(group) + 1 for group in peers[:stage])] = value
+        for index in range(len(peers[stage])):
+            gain_copy(stage, index).start()
+
+    def gain_step(stage):
+        base = sum(len(group) + 1 for group in peers[:stage])
+        total = r["gain_buf"][base]
+        for index in range(len(peers[stage])):
+            gain_copy(stage, index).wait_recv()
+            total = total + r["gain_buf"][base + 1 + index]
+        if stage + 1 < len(peers):
+            gain_start(stage + 1, total)
+            return
+        for row, name in enumerate(("gain_attn_sum", "gain_mlp_sum")):
+            for j in range(width // 128):
+                r[name][j : j + 1, :] = total[row : row + 1, 128 * j : 128 * (j + 1)]
 
     def arrivals(point):
         for name, level, first in schedule.get(point, ()):
@@ -460,7 +516,7 @@
 
     act, other = r["act"], r["other"]
     load_tokens.wait()
-    pl.semaphore_wait(barrier, bits + 3)
+    pl.semaphore_wait(barrier, len(greeted))
     pl.when(position < devices - 1)(halo_out.start)
     first_norm(r["x"], act)
     load_out.start()
@@ -572,24 +628,26 @@
             for copy in hidden_weights(at + depth, at + depth):
                 copy.start()
 
-    early = (("gate", "dgate"), ("up", "dup"))
     early_factors = {}
+
+    def early(at):
+        return [
+            (name, at - part[1]) for name, part in PARTS.items() if part[0] in ("gate", "up") and part[1] <= at < part[2]
+        ]
 
     def wait_chunk(at):
         if at >= 0:
             pair_chunk(at).wait_recv()
 
     def form_chunk(at):
-        if at >= 0:
-            for name, _ in early:
-                if name not in early_factors:
-                    early_factors[name] = factors(name, half)
-                r["send_" + name][at] = product(early_factors[name], at).astype(BF16)
+        for name, place in early(at):
+            if name not in early_factors:
+                early_factors[name] = factors(name, half)
+            r["send_" + name][place] = product(early_factors[name], at).astype(BF16)
 
     def send_chunk(at):
-        if at >= 0:
-            for name, _ in early:
-                step_copy(name, 0, at, at + 1).start()
+        for name, place in early(at):
+            step_copy(name, 0, place, place + 1).start()
 
     load_cot.wait()
     for copy in load_tails:
@@ -617,8 +675,9 @@
         wait_chunk(at)
         form_chunk(at)
         send_chunk(at)
-    send_products("down")
-    send_products("rest")
+    for name, part in PARTS.items():
+        if part[0] == "down":
+            send_products(name)
 
 
     sums = [pl.ds(n * CHUNK, CHUNK) for n in range(2 * chunks)]
@@ -719,9 +778,6 @@
         arrivals("attend" + str(at))
     for name in ("dquery", "dkeyval", "dkvback"):
         pair[name].start()
-    send_products("out")
-    arrivals("out")
-
     def through_keys(ref, at):
         return dot_rows(ref[0, :, :width], r["ring_up"][at]) + dot_rows(ref[0, :, width:], r["ring_down"][at])
 
@@ -738,41 +794,44 @@
     loop(0, chunks, back_chunk)
     pl.when(position > 0)(halo_back.start)
     arrivals("back")
-    send_products("query")
-    arrivals("query")
-    send_products("keyval")
-    arrivals("keyval")
+    send_products("out")
+    arrivals("out")
+
+    def gain_parts(at, gain_sum):
+        rows = some_rows(at)
+        for grad, name in ((summed(at, 0), "x"), (r["back_out"][rows, :].astype(F32), "x_before")):
+            value = r[name][rows, :].astype(F32)
+            gain_sum = gain_sum + jnp.sum(grad * (value * row_scale(value)), axis=0, keepdims=True)
+        return gain_sum
+
+    for name in ("query", "key", "keyb"):
+        send_products(name)
+        arrivals(name)
     loop(0, chunks, first_chunk)
+    gain_attn_sum = lax.fori_loop(0, micro, gain_parts, jnp.zeros((1, width), F32))
+    gain_start(0, jnp.concatenate([gain_attn_sum, gain_mlp_sum, jnp.zeros((6, width), F32)], axis=0))
     arrivals("first")
 
-
-    def input_backward(at, gain_sum):
+    def input_backward(at):
         rows = some_rows(at)
         back = jnp.where(position < devices - 1, r["back_in"][rows, :].astype(F32), 0.0)
-        grad = summed(at, 0) + back
-        grad, part = norm_backward(grad, r["x"][rows, :].astype(F32), r["gain_attn"][...])
+        grad, _ = norm_backward(summed(at, 0) + back, r["x"][rows, :].astype(F32), r["gain_attn"][...])
         middle[rows, :] = middle[rows, :] + grad
-        return gain_sum + part
-
+
+    for stage in range(len(peers)):
+        gain_step(stage)
+        arrivals("gain" + str(stage))
     pl.when(position < devices - 1)(halo_back.wait_recv)
-    gain_attn_sum = lax.fori_loop(0, micro, input_backward, jnp.zeros((1, width), F32))
-    r["gain_buf"][0] = jnp.concatenate([gain_attn_sum, gain_mlp_sum, jnp.zeros((6, width), F32)], axis=0)
-    gain_copy(0).start()
-    arrivals("input")
-    for bit in range(bits - 1):
-        gain_step(bit)
-        arrivals("gain" + str(bit))
-    gain_step(bits - 1)
-    arrivals("gain" + str(bits - 1))
-    gain_step(bits)
+    loop(0, micro, input_backward)
     arrivals("last")
 
     pl.when(position < devices - 1)(halo_out.wait_send)
     pl.when(position > 0)(halo_back.wait_send)
     for copy in pair.values():
         copy.wait_send()
-    for bit in range(bits + 1):
-        gain_copy(bit).wait_send()
+    for stage, group in enumerate(peers):
+        for index in range(len(group)):
+            gain_copy(stage, index).wait_send()
     pair_chunk(0, full + 1).wait_send()
     for name in PARTS:
         for level in range(bits):
@@ -836,7 +895,7 @@
         "hidden": pltpu.VMEM((rows_all, padded), BF16),
         "columns": pltpu.VMEM((padded, rows_all), F32),
         "square": pltpu.VMEM((rows_all, CHUNK), F32),
-        "gain_buf": pltpu.VMEM((2 * bits + 2, 8, width), F32),
+        "gain_buf": pltpu.VMEM((stage_copies(bits) + 3, 8, width), F32),
     }
     for name in ROWS:
         scratch["row_" + name] = pltpu.VMEM((count, 2, unit_rows[name], rows_all), BF16)
@@ -845,19 +904,19 @@
         if name not in CHUNKED:
             scratch["col_" + name] = pltpu.VMEM((2, rows_all, widths[name]), BF16)
     scratch["col_hidden"] = pltpu.VMEM((2, padded // CHUNK, len(CHUNKED), rows_all, CHUNK), BF16)
-    for name, (matrix, first, last, _) in PARTS.items():
+    for name, (matrix, first, last, _, _) in PARTS.items():
         rows = unit_rows[MATRICES[matrix][0][0]]
         scratch["send_" + name] = pltpu.VMEM((last - first, half, rows, CHUNK), BF16)
         for level in range(bits):
             scratch[f"land_{name}{level}"] = pltpu.VMEM((last - first, half >> level, rows, CHUNK), BF16)
-        if name in ("gate", "up"):
-            scratch["turn_" + name] = pltpu.VMEM(((last - first) * CHUNK // 128 * rows, 128), F32)
+        if matrix in ("gate", "up"):
+            scratch["turn_" + matrix] = pltpu.VMEM((padded // 128 * rows, 128), F32)
         else:
             scratch["total_" + name] = pltpu.VMEM((last - first, rows, CHUNK), F32)
     sems = {"local_sem": (6,), "ring_sem": (3, depth)}
     sems.update(chunk_send=(1,), chunk_recv=(padded // CHUNK,))
     sems.update(step_send=(len(PARTS), bits), step_recv=(step_layout(bits)[1],))
-    for name, number in (("pair", len(ROWS) + len(COLS) - len(CHUNKED)), ("halo", 2), ("gain", bits + 1)):
+    for name, number in (("pair", len(ROWS) + len(COLS) - len(CHUNKED)), ("halo", 2), ("gain", stage_copies(bits))):
         sems[name + "_send"] = sems[name + "_recv"] = (number,)
     for name, shape in sems.items():
         scratch[name] = pltpu.SemaphoreType.DMA(shape)

time: 162 us -> 148 us (0.914)
  Pallas kernels: 161 us -> 147 us
    pallas_call x1, Pallas kernels: 158 us -> 144 us  [layer(): pl.pallas_call(functools.partial(layer_kernel, sizes, tuple(inputs), tupl...]
where the time goes in v4:
time: 148 us
  Pallas kernels  147 us (99%)
    pallas_call x1, Pallas kernels, layer(): pl.pallas_call(functools.partial(layer_kernel, sizes, tuple(inputs), tupl...  144 us
    pallas_call x1, Pallas kernels, handed_on(): pl.pallas_call(functools.partial(hand_on_kernel, count), out_shape=[jax.S...  3.08 us

profile of v4, /device:TPU:0, one launch (start us, length us, event | category | flops | bytes accessed | tf_op | source)
XLA Modules:
  0.0 148.2 jit_solution(5675635256917205082)
XLA Ops:
  0.6 144.3 %layer.1 = (bf16[256,1024]{1,0:T(8,128)(2,1)}, f32[256,1024]{1,0:T(8,128)}, f32[8,128]{1,0:T(8,128)}, f32[8,128]{1,0:T(8,128)}, f32[256,128]{1,0:T(8,128)}, /*in...) custom-call(bf16[256,1024]{1,0:T(8,128)(2,1)} %bitcast.19, ...), custom_call_target="tpu_custom_call" | custom-call | tf_op jit(solution)/shard_map/layer/pallas_call | solution.py:925
  145.0 3.1 %hand_on.1 = (bf16[256,1024]{1,0:T(8,128)(2,1)}, f32[256,1024]{1,0:T(8,128)}, f32[8,128]{1,0:T(8,128)}, f32[8,128]{1,0:T(8,128)}, f32[256,128]{1,0:T(8,128)}, /*...) custom-call(bf16[256,1024]{1,0:T(8,128)(2,1)} %get-tuple-element.33., ...), custom_call_target="tpu_custom_call" | custom-call | tf_op jit(solution)/shard_map/hand_on/pallas_call | solution.py:962
